TPU v7x, 256 devices: a whole 4x4x8 slice. The times are simulated.
256 devices in a mesh: row: 16 (over z, core), col: 16 (over y, x).
Axes of the slice: x: 4, y: 4, z: 8, core: 2. Of those that a mesh axis runs over, the one named last changes fastest.
Arguments:
- front: float32 [24576, 24576], P('row', 'col')
- panel_one: float32 [24576, 256], P('row'), may hold values from -0.0012207031 to 0.0012207031
- panel_two: float32 [24576, 256], P('row'), may hold values from -0.00030517578 to 0.00030517578
- lower_one: float32 [256, 256], replicated, may hold values from -0.375 to 0.375
- lower_two: float32 [256, 256], replicated, may hold values from -0.375 to 0.375
- pivot_one: float32 [256, 256], replicated, may hold values from -4 to 4
- pivot_two: float32 [256, 256], replicated, may hold values from -4 to 4
- rows_one: int32 [12288], replicated, may hold values from 0 to 24575, as said below
- rows_two: int32 [8192], replicated, may hold values from 0 to 24575, as said below
Outputs:
- panel_inverse_one: float32 [24576, 256], P(('row', 'col'))
- diag_inverse_one: float32 [256, 256], replicated
- panel_inverse_two: float32 [24576, 256], P(('row', 'col'))
- diag_inverse_two: float32 [256, 256], replicated
Inputs may be any that keep to these rules, and one draw needn't show every extreme that they name: `rows_one`: 12288 distinct indices in increasing order; 0 and 24575 are among them. `rows_two`: 8192 distinct indices in increasing order; 0 and 24575 are among them.
All inputs are finite; a program needn't handle non-finite values.
Results may differ from a plain program's by a relative error of at most 0.000078.
Values sent between devices are 32-bit elements; how exact they have to be, the bound alone decides.
No kernel may reach another device: no remote copies, remote signals or barrier semaphores. Data moves between devices by JAX's collectives and lax.ppermute only.
A program may use at most 64 MiB of HBM per device.

v0:
```python
import jax
import jax.numpy as jnp
from jax import lax
from jax.sharding import PartitionSpec as P

HIGHEST = lax.Precision.HIGHEST


def from_root(block, axis, holder):
    block = jnp.where(lax.axis_index(axis) == holder, block, jnp.zeros_like(block))
    return lax.psum(block, axis)


def matmul(left, right):
    return jnp.dot(left, right, precision=HIGHEST, preferred_element_type=jnp.float32)


def inner(left, right):
    return lax.dot_general(
        left, right, (((0,), (0,)), ((), ())), precision=HIGHEST, preferred_element_type=jnp.float32
    )


def per_device(
    front, panel_one, panel_two, lower_one, lower_two, pivot_one, pivot_two, rows_one, rows_two
):
    row_count = lax.axis_size("row")
    col_count = lax.axis_size("col")
    row_place = lax.axis_index("row")
    col_place = lax.axis_index("col")
    row_block = front.shape[0]
    col_block = front.shape[1]
    order_full = row_block * row_count
    piece = row_block // col_count

    def selected(rows):
        return jnp.zeros((order_full,), jnp.float32).at[rows].set(1.0)

    def column_block(local):
        first = col_place * col_block // row_block
        pieces = from_root(local, "row", first + 0)
        return pieces

    def supernode(solved_rows, solved_cols, marks, pivot):
        mine = lax.dynamic_slice_in_dim(marks, row_place * row_block + col_place * piece, piece, 0)
        summed = lax.psum_scatter(
            matmul(front, solved_cols), "col", scatter_dimension=0, tiled=True
        )
        inverse_panel = -(mine[:, None] * summed)
        owned = lax.dynamic_slice_in_dim(solved_rows, col_place * piece, piece, 0)
        total = lax.psum(inner(owned, inverse_panel), ("row", "col"))
        inverse_diag = pivot - total
        return (inverse_panel, inverse_diag)

    marks_one = selected(rows_one)
    marks_two = selected(rows_two)
    local_one = lax.dynamic_slice_in_dim(marks_one, row_place * row_block, row_block, 0)
    local_two = lax.dynamic_slice_in_dim(marks_two, row_place * row_block, row_block, 0)
    solved_one = matmul(local_one[:, None] * panel_one, lower_one)
    cols_one = column_block(solved_one)
    base_two = matmul(local_two[:, None] * panel_two, lower_two)
    panel_inverse_one, diag_inverse_one = supernode(solved_one, cols_one, marks_one, pivot_one)
    solved_two = matmul(base_two, diag_inverse_one)
    cols_two = column_block(solved_two)
    panel_inverse_two, diag_inverse_two = supernode(solved_two, cols_two, marks_two, pivot_two)
    return (panel_inverse_one, diag_inverse_one, panel_inverse_two, diag_inverse_two)


def solution(mesh):
    in_specs = (P("row", "col"), P("row", None), P("row", None), P(), P(), P(), P(), P(), P())
    out_specs = (P(("row", "col"), None), P(), P(("row", "col"), None), P())
    return jax.shard_map(
        per_device, mesh=mesh, in_specs=in_specs, out_specs=out_specs, check_vma=False
    )
```

profile of v0, /device:TPU:1, one launch (start us, length us, event | category | flops | bytes accessed | tf_op | source)
XLA Modules:
  0.0 1007.5 jit_solution(3761977828783623531)
XLA Ops:
  7.2 0.0 copy-start
  7.2 0.0 all-reduce.5.cloned.1.call-start
  7.3 0.8 compare_select_fusion
  8.1 45.4 %scatter_custom_fusion = f32[24576]{0:T(1024)S(1)} fusion(s32[12288]{0:T(1024)S(1)} %compare_select_fusion, f32[12288]{0:T(1024)S(1)} %broadcast.12, f32[]{:T(128)} %constant.10.clone.1), kind=kCustom, calls=%fused_computation.22 | custom fusion | bytes 98308 | tf_op jit(solution)/shard_map/scatter | solution.py:37
  53.5 0.1 dynamic_slice.19
  53.6 0.0 copy-done
  53.6 4.0 broadcast_select_fusion.1
  57.6 0.0 all-reduce.5.cloned.1.call-update
  57.6 0.0 reduce-scatter.7.cloned.1.call-start
  57.7 116.9 %all-reduce.5.cloned.1.call-done = f32[1536,256]{1,0:T(8,128)} async-done(((f32[1536,256]{1,0:T(8,128)}), f32[1536,256]{1,0:T(8,128)}) %all-reduce.5.cloned.1.call-update) | async-done | bytes 1572880 | tf_op jit(solution)/shard_map/psum | solution.py:11
  174.6 18.0 %convolution_bitcast_fusion.1 = f32[1536,256]{0,1:T(8,128)S(1)} fusion(f32[1536,256]{1,0:T(8,128)} %all-reduce.5.cloned.1.call-done, f32[1536,1536]{1,0:T(8,128)} %param.9), kind=kOutput, calls=%fused_computation.3 | convolution fusion | flops 7247757312 | bytes 12582912 | tf_op jit(solution)/shard_map/dot_general | solution.py:15
  192.7 1.6 copy.17
  194.3 0.0 reduce-scatter.7.cloned.1.call-update
  194.3 0.0 all-reduce.7.cloned.1.call-start
  194.4 0.1 dynamic_slice.18
  194.5 0.6 copy-done.5
  195.1 30.7 %scatter_custom_fusion.1 = f32[24576]{0:T(1024)S(1)} fusion(s32[8192]{0:T(1024)S(1)} %compare_select_fusion.1, f32[8192]{0:T(1024)S(1)} %broadcast.13, f32[]{:T(128)} %constant.10.clone.1), kind=kCustom, calls=%fused_computation.20 | custom fusion | bytes 98308 | tf_op jit(solution)/shard_map/scatter | solution.py:37
  225.8 0.0 copy-start.4
  225.8 0.1 dynamic_slice.22
  225.9 0.5 copy-done.4
  226.4 45.6 %reduce-scatter.7.cloned.1.call-done = f32[96,256]{1,0:T(8,128)} async-done(((f32[1536,256]{1,0:T(8,128)}), f32[96,256]{1,0:T(8,128)}) %reduce-scatter.7.cloned.1.call-update) | async-done | bytes 98320
  272.0 1.0 copy.18
  273.0 1.1 fusion.8
  274.1 0.0 all-reduce.7.cloned.1.call-update
  274.1 0.0 copy-start.2
  274.1 0.0 all-reduce.9.cloned.1.call-start
  274.2 2.9 fusion
  277.1 251.7 %all-reduce.7.cloned.1.call-done = f32[256,256]{1,0:T(8,128)} async-done(((f32[256,256]{1,0:T(8,128)}), f32[256,256]{1,0:T(8,128)}) %all-reduce.7.cloned.1.call-update) | async-done | bytes 262160 | tf_op jit(solution)/shard_map/psum | solution.py:51
  528.8 1.0 sub.12
  529.8 0.0 copy-start.1
  529.8 2.6 broadcast_select_fusion
  532.4 0.0 copy-done.1
  532.4 0.0 all-reduce.9.cloned.1.call-update
  532.4 0.0 reduce-scatter.9.cloned.1.call-start
  532.5 113.4 %all-reduce.9.cloned.1.call-done = f32[1536,256]{1,0:T(8,128)} async-done(((f32[1536,256]{1,0:T(8,128)}), f32[1536,256]{1,0:T(8,128)}) %all-reduce.9.cloned.1.call-update) | async-done | bytes 1572880 | tf_op jit(solution)/shard_map/psum | solution.py:11
  645.8 18.0 %convolution_bitcast_fusion = f32[1536,256]{0,1:T(8,128)S(1)} fusion(f32[1536,256]{1,0:T(8,128)} %all-reduce.9.cloned.1.call-done, f32[1536,1536]{1,0:T(8,128)} %param.9), kind=kOutput, calls=%fused_computation.2 | convolution fusion | flops 7247757312 | bytes 12582912 | tf_op jit(solution)/shard_map/dot_general | solution.py:15
  663.9 1.6 copy.19
  665.5 0.0 reduce-scatter.9.cloned.1.call-update
  665.5 0.0 all-reduce.11.cloned.1.call-start
  665.6 0.8 dynamic_slice.21
  666.4 76.7 %reduce-scatter.9.cloned.1.call-done = f32[96,256]{1,0:T(8,128)} async-done(((f32[1536,256]{1,0:T(8,128)}), f32[96,256]{1,0:T(8,128)}) %reduce-scatter.9.cloned.1.call-update) | async-done | bytes 98320
  743.1 1.0 copy.20
  744.1 1.1 fusion.6
  745.3 0.0 all-reduce.11.cloned.1.call-update
  745.3 0.7 copy.15
  746.0 0.7 copy.16
  746.7 252.3 %all-reduce.11.cloned.1.call-done = f32[256,256]{1,0:T(8,128)} async-done(((f32[256,256]{1,0:T(8,128)}), f32[256,256]{1,0:T(8,128)}) %all-reduce.11.cloned.1.call-update) | async-done | bytes 262160 | tf_op jit(solution)/shard_map/psum | solution.py:51
  999.0 1.7 sub.13
  (9 shorter events, 0.0 us)
Async XLA Ops:
  7.2 46.4 %copy-start = (f32[256,256]{1,0:T(8,128)S(1)}, f32[256,256]{1,0:T(8,128)}, u32[]{:S(2)}) copy-start(f32[256,256]{1,0:T(8,128)} %param.12) | copy-start | bytes 786436
  7.2 167.4 %all-reduce.5.cloned.1.call-start = ((), (), s32[]{:S(2)}) async-start(), calls=%async_computation.2 | async-start | bytes 3145728 | tf_op jit(solution)/shard_map/psum | solution.py:11
  57.6 214.3 %reduce-scatter.7.cloned.1.call-start = ((), (), s32[]{:S(2)}) async-start(), calls=%async_computation.6 | async-start | bytes 1671168
  194.3 0.8 copy-start.5
  194.3 334.5 %all-reduce.7.cloned.1.call-start = ((), (), s32[]{:S(2)}) async-start(), calls=%async_computation.3 | async-start | bytes 524288 | tf_op jit(solution)/shard_map/psum | solution.py:51
  225.8 0.6 copy-start.4
  274.1 254.7 %copy-start.2 = (f32[256,256]{1,0:T(8,128)S(1)}, f32[256,256]{1,0:T(8,128)}, u32[]{:S(2)}) copy-start(f32[256,256]{1,0:T(8,128)} %param.14) | copy-start | bytes 786436
  274.1 371.7 %all-reduce.9.cloned.1.call-start = ((), (), s32[]{:S(2)}) async-start(), calls=%async_computation.4 | async-start | bytes 3145728 | tf_op jit(solution)/shard_map/psum | solution.py:11
  529.8 2.6 copy-start.1
  532.4 210.7 %reduce-scatter.9.cloned.1.call-start = ((), (), s32[]{:S(2)}) async-start(), calls=%async_computation.7 | async-start | bytes 1671168
  665.5 333.5 %copy-start.3 = (f32[256,256]{1,0:T(8,128)S(1)}, f32[256,256]{1,0:T(8,128)}, u32[]{:S(2)}) copy-start(f32[256,256]{1,0:T(8,128)} %param.15) | copy-start | bytes 786436
  665.5 333.4 %all-reduce.11.cloned.1.call-start = ((), (), s32[]{:S(2)}) async-start(), calls=%async_computation.5 | async-start | bytes 524288 | tf_op jit(solution)/shard_map/psum | solution.py:51
Sparse Core Ops, SparseCore 0:
  57.7 116.8 all-reduce.4
  194.4 77.4 reduce-scatter.6
  278.9 249.8 all-reduce.6
  532.5 113.2 all-reduce.8
  665.7 77.4 reduce-scatter.8
  749.0 249.9 all-reduce.10
where the time goes:
time: 1010 us
  waiting for transfers between devices  857 us (85%)
  local copies, waits for them, and re-layouts  85 us (8%)
  matrix products  47.8 us (5%)
  between operations  14.3 us (1%)
    psum x2, waiting for transfers between devices, supernode(): total = lax.psum(inner(owned, inverse_panel), ('row', 'col'))  504 us
    psum x2, waiting for transfers between devices, from_root(): return lax.psum(block, axis)  230 us
    unnamed x8, waiting for transfers between devices  122 us
    scatter x2, local copies, waits for them, and re-layouts, selected(): return jnp.zeros((order_full,), jnp.float32).at[rows].set(1.0)  76.1 us
    dot_general x5, matrix products, matmul(): jnp.dot(left, right, precision=HIGHEST, preferred_element_type=jnp.float32)  45.5 us
  transfers between devices with their start and end apart: 6, of which 6 were waited for; matrix products, arithmetic and copies ran while one was open for 4% of the time, Pallas kernels for 0%

commit v1 on v0

v1 whole, which is shorter than its diff:
```python
import functools

import jax
import jax.numpy as jnp
from jax import lax
from jax.experimental import pallas as pl
from jax.experimental.pallas import tpu as pltpu
from jax.sharding import PartitionSpec as P

HIGHEST = lax.Precision.HIGHEST
F32 = jnp.float32
BF16 = jnp.bfloat16
NT = (((1,), (1,)), ((), ()))
NN = (((1,), (0,)), ((), ()))
STEPS = 4
PIECE = 96
SLOTS = 112


def split(x):
    hi = x.astype(BF16)
    return hi, (x - hi.astype(F32)).astype(BF16)


def dot3(left, right, dims=NN):
    (lh, ll), (rh, rl) = left, right
    dot = functools.partial(lax.dot_general, dimension_numbers=dims, preferred_element_type=F32)
    return dot(lh, rh) + (dot(lh, rl) + dot(ll, rh))


def matmul(left, right):
    return jnp.dot(left, right, precision=HIGHEST, preferred_element_type=F32)


def one_hot(values, count):
    return jnp.where(values == lax.broadcasted_iota(jnp.int32, (count, values.shape[1]), 0), 1.0, 0.0).astype(BF16)


def one_dot(left, right, dims=NN):
    return lax.dot_general(left, right, dims, preferred_element_type=F32)


def local_kernel(
    place, rows_one, rows_two, panel_one, panel_two, lt_one, lt_two, hi, lo, slots, slots_t, counts
):
    earlier = lax.broadcasted_iota(jnp.int32, (PIECE, PIECE), 0) < lax.broadcasted_iota(jnp.int32, (PIECE, PIECE), 1)
    earlier = jnp.where(earlier, 1.0, 0.0).astype(BF16)
    later = lax.broadcasted_iota(jnp.int32, (PIECE, PIECE), 1) < lax.broadcasted_iota(jnp.int32, (PIECE, PIECE), 0)
    later = jnp.where(later, 1.0, 0.0).astype(BF16)
    before, before_t, length = [0.0, 0.0], [0.0, 0.0], 0.0
    for at, (rows, panel, lt) in enumerate(((rows_one, panel_one, lt_one), (rows_two, panel_two, lt_two))):
        index = rows[...]
        piece = lax.shift_right_logical(lax.shift_right_logical(index, 5) * 43691, 17)
        low = one_hot(index - PIECE * piece, PIECE)
        block = lax.shift_right_logical(piece, 4)
        inner = lax.bitwise_and(piece, 15)
        length = length + one_dot(one_hot(block, 16), one_hot(inner, 16), NT)
        for which in range(2):
            mine = one_hot(jnp.where(block == place[which], inner, -1), 16)
            marks = one_dot(mine, low, NT)
            slot = one_dot(marks.astype(BF16), earlier) + before[which]
            slots[which, at] = jnp.where(marks > 0.5, slot, -1.0)
            before[which] = before[which] + jnp.sum(marks, axis=1, keepdims=True)
            marks_t = one_dot(low, mine, NT)
            slot = one_dot(later, marks_t.astype(BF16)) + before_t[which]
            slots_t[which, at] = jnp.where(marks_t > 0.5, slot, -1.0)
            before_t[which] = before_t[which] + jnp.sum(marks_t, axis=0, keepdims=True)
            if which == 0:
                chosen = [panel[PIECE * j:PIECE * j + PIECE, :] * marks_t[:, j:j + 1] for j in range(16)]
                h, l = split(dot3(split(lt[...]), split(jnp.concatenate(chosen, axis=0)), NT))
                hi[at] = h
                lo[at] = l
    counts[...] = length


def local_solved(place, rows_one, rows_two, panel_one, panel_two, lower_one, lower_two):
    block, sn = panel_one.shape
    vmem = pl.BlockSpec(memory_space=pltpu.VMEM)
    return pl.pallas_call(
        local_kernel,
        out_shape=[jax.ShapeDtypeStruct((2, sn, block), BF16)] * 2
        + [
            jax.ShapeDtypeStruct((2, 2, 16, PIECE), F32),
            jax.ShapeDtypeStruct((2, 2, PIECE, 16), F32),
            jax.ShapeDtypeStruct((16, 16), F32),
        ],
        in_specs=[pl.BlockSpec(memory_space=pltpu.SMEM)] + [vmem] * 6,
        out_specs=[vmem] * 5,
        compiler_params=pltpu.CompilerParams(vmem_limit_bytes=56 << 20),
        cost_estimate=pl.CostEstimate(flops=6_000_000_000, bytes_accessed=8_000_000, transcendentals=0),
    )(place, rows_one[None, :], rows_two[None, :], panel_one, panel_two, lower_one.T, lower_two.T)


def gather_matrix(slot):
    wanted = lax.broadcasted_iota(jnp.int32, (SLOTS, PIECE), 0).astype(F32)
    return jnp.where(slot == wanted, 1.0, 0.0).astype(BF16)


def scatter_matrix(slot):
    wanted = lax.broadcasted_iota(jnp.int32, (PIECE, SLOTS), 1).astype(F32)
    return jnp.where(slot == wanted, 1.0, 0.0).astype(BF16)


def pack(slot_one, slot_two, block_one, block_two):
    total = None
    for slot, block in ((slot_one, block_one), (slot_two, block_two)):
        chosen = gather_matrix(slot)
        hi, lo = split(block)
        part = one_dot(chosen, hi) + one_dot(chosen, lo)
        total = part if total is None else total + part
    return total


def piece_kernel(at, got, slots, lower_one, lower_two, out):
    sn = lower_one.shape[0]
    solved = [
        dot3(split(got[:, :sn]), split(lower_one[...])),
        dot3(split(got[:, sn:]), split(lower_two[...])),
    ]
    packed = pack(slots[1, 0, pl.ds(at[0], 1), :], slots[1, 1, pl.ds(at[0], 1), :], *solved)
    for copy in range(out.shape[0]):
        out[copy] = packed


def packed_piece(at, got, slots, lower_one, lower_two, copies):
    vmem = pl.BlockSpec(memory_space=pltpu.VMEM)
    return pl.pallas_call(
        piece_kernel,
        out_shape=jax.ShapeDtypeStruct((copies, SLOTS, lower_one.shape[0]), F32),
        in_specs=[pl.BlockSpec(memory_space=pltpu.SMEM)] + [vmem] * 4,
        out_specs=vmem,
        compiler_params=pltpu.CompilerParams(vmem_limit_bytes=48 << 20),
        cost_estimate=pl.CostEstimate(flops=200_000_000, bytes_accessed=2_000_000, transcendentals=0),
    )(at, got, slots, lower_one, lower_two)


def packed_front_kernel(core, front, own, other, slots_t, slots, st_hi, st_lo, out, s_hi, s_lo, diag):
    step = pl.program_id(0)
    half = s_hi.shape[1]
    sn = st_hi.shape[1]
    tile = front.shape[0]
    pieces = tile // PIECE

    @pl.when(step == 0)
    def _():
        for at, ref in enumerate((own, other)):
            first = (core[0] if at == 0 else 1 - core[0]) == 0
            for which in range(2):
                slot = slots_t[1, which]
                slot = jnp.where(first, slot[:, :8], slot[:, 8:])
                for p in range(8):
                    place = scatter_matrix(slot[:, p:p + 1])
                    h, l = split(ref[p])
                    into = (at, slice(PIECE * p, PIECE * p + PIECE), slice(sn * which, sn * which + sn))
                    s_hi[into] = one_dot(place, h).astype(BF16)
                    s_lo[into] = one_dot(place, l).astype(BF16)
        diag[...] = jnp.zeros_like(diag)

    total = None
    for at in range(2):
        which = core[0] if at == 0 else 1 - core[0]
        columns = pl.ds(pl.multiple_of(which * half, half), half)
        part = dot3(split(front[:, columns]), (s_hi[at], s_lo[at]))
        total = part if total is None else total + part
    for p in range(pieces):
        now = pieces * step + p
        rows = slice(PIECE * p, PIECE * p + PIECE)
        out[now, :SLOTS, :] = pack(
            slots[0, 0, pl.ds(now, 1), :], slots[0, 1, pl.ds(now, 1), :], total[rows, :sn], total[rows, sn:]
        )
    for at in range(2):
        diag[at] += dot3((st_hi[at], st_lo[at]), split(total[:, sn * at:sn * at + sn]))

    @pl.when(step == STEPS - 1)
    def _():
        share = sn // out.shape[0]
        for d in range(out.shape[0]):
            for at in range(2):
                out[d, SLOTS + share * at:SLOTS + share * at + share, :] = diag[at, share * d:share * d + share, :]


def packed_front_product(core, front, own, other, slots_t, slots, st_hi, st_lo, col_count):
    rows, cols = front.shape
    sn = own.shape[2]
    tile = rows // STEPS
    whole = lambda a: pl.BlockSpec(a.shape, lambda i: (0,) * a.ndim)
    out = (col_count, SLOTS + 2 * (sn // col_count), sn)
    return pl.pallas_call(
        packed_front_kernel,
        grid=(STEPS,),
        out_shape=jax.ShapeDtypeStruct(out, F32),
        in_specs=[
            pl.BlockSpec(memory_space=pltpu.SMEM),
            pl.BlockSpec((tile, cols), lambda i: (i, 0)),
            whole(own), whole(other), whole(slots_t), whole(slots),
            pl.BlockSpec((2, sn, tile), lambda i: (0, 0, i)),
            pl.BlockSpec((2, sn, tile), lambda i: (0, 0, i)),
        ],
        out_specs=pl.BlockSpec(out, lambda i: (0, 0, 0)),
        scratch_shapes=[
            pltpu.VMEM((2, cols // 2, 2 * sn), BF16),
            pltpu.VMEM((2, cols // 2, 2 * sn), BF16),
            pltpu.VMEM((2, sn, sn), F32),
        ],
        compiler_params=pltpu.CompilerParams(vmem_limit_bytes=56 << 20),
        cost_estimate=pl.CostEstimate(flops=12 * rows * cols * sn, bytes_accessed=20_000_000, transcendentals=0),
    )(core, front, own, other, slots_t, slots, st_hi, st_lo)


def sum_kernel(at, parts, slots_t, inverse_one, product_two, shares):
    total = parts[0]
    for d in range(1, parts.shape[0]):
        total = total + parts[d]
    shares[...] = total[SLOTS:, :]
    hi, rest = total[:SLOTS, :].astype(BF16), total[:SLOTS, :]
    rest = rest - hi.astype(F32)
    mid = rest.astype(BF16)
    low = (rest - mid.astype(F32)).astype(BF16)
    for which in range(2):
        slot = slots_t[0, which]
        picked = lax.broadcasted_iota(jnp.int32, slot.shape, 1) == at[0]
        place = scatter_matrix(jnp.sum(jnp.where(picked, slot, 0.0), axis=1, keepdims=True))
        rows = one_dot(place, hi) + (one_dot(place, mid) + one_dot(place, low))
        if which == 0:
            inverse_one[...] = -rows
        else:
            product_two[...] = rows


def summed_piece(at, parts, slots_t):
    sn = parts.shape[2]
    vmem = pl.BlockSpec(memory_space=pltpu.VMEM)
    return pl.pallas_call(
        sum_kernel,
        out_shape=[jax.ShapeDtypeStruct((PIECE, sn), F32)] * 2
        + [jax.ShapeDtypeStruct((parts.shape[1] - SLOTS, sn), F32)],
        in_specs=[pl.BlockSpec(memory_space=pltpu.SMEM), vmem, vmem],
        out_specs=[vmem] * 3,
        compiler_params=pltpu.CompilerParams(vmem_limit_bytes=48 << 20),
        cost_estimate=pl.CostEstimate(flops=100_000_000, bytes_accessed=3_000_000, transcendentals=0),
    )(at, parts, slots_t)


def front_kernel(core, front, own, other, st_hi, st_lo, out, s_hi, s_lo, diag):
    step = pl.program_id(0)
    half = own.shape[0]
    sn = st_hi.shape[1]
    tile = front.shape[0]
    pieces = tile // 96

    @pl.when(step == 0)
    def _():
        for at, ref in enumerate((own, other)):
            h, l = split(ref[...])
            s_hi[at] = h
            s_lo[at] = l
        diag[...] = jnp.zeros_like(diag)

    total = None
    for at in range(2):
        which = core[0] if at == 0 else 1 - core[0]
        columns = pl.ds(pl.multiple_of(which * half, half), half)
        part = dot3(split(front[:, columns]), (s_hi[at], s_lo[at]))
        total = part if total is None else total + part
    for p in range(pieces):
        out[pieces * step + p, :96, :] = total[96 * p:96 * p + 96, :]
    for at in range(2):
        cols = slice(sn * at, sn * at + sn)
        diag[:, cols] += dot3((st_hi[at], st_lo[at]), split(total[:, cols]))

    @pl.when(step == STEPS - 1)
    def _():
        share = sn // out.shape[0]
        for d in range(out.shape[0]):
            out[d, 96:, :] = diag[share * d:share * d + share, :]


def front_product(core, front, own, other, st_hi, st_lo, col_count):
    rows, cols = front.shape
    wide = own.shape[1]
    sn = wide // 2
    tile = rows // STEPS
    whole = lambda a: pl.BlockSpec(a.shape, lambda i: (0,) * a.ndim)
    out = (col_count, rows // col_count + sn // col_count, wide)
    return pl.pallas_call(
        front_kernel,
        grid=(STEPS,),
        out_shape=jax.ShapeDtypeStruct(out, F32),
        in_specs=[
            pl.BlockSpec(memory_space=pltpu.SMEM),
            pl.BlockSpec((tile, cols), lambda i: (i, 0)),
            whole(own), whole(other),
            pl.BlockSpec((2, sn, tile), lambda i: (0, 0, i)),
            pl.BlockSpec((2, sn, tile), lambda i: (0, 0, i)),
        ],
        out_specs=pl.BlockSpec(out, lambda i: (0, 0, 0)),
        scratch_shapes=[
            pltpu.VMEM((2, cols // 2, wide), BF16),
            pltpu.VMEM((2, cols // 2, wide), BF16),
            pltpu.VMEM((sn, wide), F32),
        ],
        compiler_params=pltpu.CompilerParams(vmem_limit_bytes=56 << 20),
        cost_estimate=pl.CostEstimate(flops=6 * rows * cols * wide, bytes_accessed=20_000_000, transcendentals=0),
    )(core, front, own, other, st_hi, st_lo)


def marked(rows, first, count):
    wanted = first + lax.broadcasted_iota(jnp.int32, (count, 1), 0)
    return jnp.any(rows[None, :] == wanted, axis=1, keepdims=True).astype(F32)


def per_device(
    front, panel_one, panel_two, lower_one, lower_two, pivot_one, pivot_two, rows_one, rows_two
):
    n = lax.axis_size("row")
    row = lax.axis_index("row")
    col = lax.axis_index("col")
    block, sn = panel_one.shape
    piece = block // n
    half = n // 2
    core = row % 2
    z = row // 2
    same_core = [list(range(0, n, 2)), list(range(1, n, 2))]
    turn = [(r * n + c, c * n + r) for r in range(n) for c in range(n)]
    swap = [(r, r ^ 1) for r in range(n)]

    def place(r):
        return (r % 2) * (block // 2) + (r // 2) * piece

    def spread(x, axis, copies, groups=None):
        return lax.all_to_all(jnp.broadcast_to(x, (copies,) + x.shape), axis, 0, 0, axis_index_groups=groups)

    sent = jnp.concatenate(
        [lax.dynamic_slice_in_dim(p, place(col), piece, 0) for p in (panel_one, panel_two)], axis=1
    )
    got = lax.ppermute(sent, ("row", "col"), turn)
    st_hi, st_lo, slots, slots_t, counts = local_solved(
        jnp.stack([row, col]), rows_one, rows_two, panel_one, panel_two, lower_one, lower_two
    )

    def packed(got, front, st_hi, st_lo, slots, slots_t):
        at = core * half + z
        mine = packed_piece(at[None], got, slots, lower_one, lower_two, half)
        own = lax.all_to_all(mine, "row", 0, 0, axis_index_groups=same_core)
        other = lax.ppermute(own, "row", swap)
        parts = packed_front_product(core[None], front, own, other, slots_t, slots, st_hi, st_lo, n)
        inverse_one, product_two, shares = summed_piece(
            col[None], lax.all_to_all(parts, "col", 0, 0), slots_t
        )
        return inverse_one, product_two, shares.reshape(2, sn // n, sn)

    def dense(got, front, st_hi, st_lo, slots, slots_t):
        first = col * block + place(row)
        solved = jnp.concatenate(
            [
                matmul(marked(rows_one, first, piece) * got[:, :sn], lower_one),
                matmul(marked(rows_two, first, piece) * got[:, sn:], lower_two),
            ],
            axis=1,
        )
        own = spread(solved, "row", half, same_core).reshape(block // 2, 2 * sn)
        other = lax.ppermute(own, "row", swap)
        parts = front_product(core[None], front, own, other, st_hi, st_lo, n)
        summed = jnp.sum(lax.all_to_all(parts, "col", 0, 0), axis=0)
        mine = row * block + col * piece
        return (
            -(marked(rows_one, mine, piece) * summed[:piece, :sn]),
            marked(rows_two, mine, piece) * summed[:piece, sn:],
            summed[piece:].reshape(sn // n, 2, sn).transpose(1, 0, 2),
        )

    inverse_one, product_two, shares = lax.cond(
        jnp.max(counts) <= SLOTS, packed, dense, got, front, st_hi, st_lo, slots, slots_t
    )

    share = (sn // n) // 2
    keep = lax.dynamic_slice_in_dim(shares, core * share, share, 1)
    give = lax.dynamic_slice_in_dim(shares, (1 - core) * share, share, 1)
    keep = keep + lax.ppermute(give, "row", swap)
    keep = jnp.sum(spread(keep, "row", half, same_core), axis=0)
    near = spread(keep, "col", n)
    far = lax.ppermute(near, "row", swap)
    diag = jnp.where(core == 0, jnp.stack([near, far], axis=2), jnp.stack([far, near], axis=2))

    diag_inverse_one = pivot_one + diag[:, 0].reshape(sn, sn)
    panel_inverse_two = -matmul(product_two, diag_inverse_one)
    right = matmul(diag[:, 1].reshape(sn, sn), diag_inverse_one)
    diag_inverse_two = pivot_two + lax.dot_general(
        diag_inverse_one, right, (((0,), (0,)), ((), ())), precision=HIGHEST, preferred_element_type=F32
    )
    return inverse_one, diag_inverse_one, panel_inverse_two, diag_inverse_two


def solution(mesh):
    in_specs = (P("row", "col"), P("row", None), P("row", None), P(), P(), P(), P(), P(), P())
    out_specs = (P(("row", "col"), None), P(), P(("row", "col"), None), P())
    return jax.shard_map(
        per_device, mesh=mesh, in_specs=in_specs, out_specs=out_specs, check_vma=False
    )
```

time: 1010 us -> 152 us (0.15)
  waiting for transfers between devices: 857 us -> 4.1 us
  blocking collectives: 0 us -> 94.9 us
  local copies, waits for them, and re-layouts: 85 us -> 5.66 us
  matrix products: 47.8 us -> 2.59 us
  Pallas kernels: 0 us -> 29.4 us
  between operations: 14.3 us -> 1.52 us
  starting transfers between devices: 0.25 us -> 10.9 us
    psum x4 -> x0, waiting for transfers between devices: 734 us -> none  [the longest x2 504 us: supernode(): total = lax.psum(inner(owned, inverse_panel), ('row', 'col'))]
    unnamed x8 -> x0, waiting for transfers between devices: 122 us -> none
    all_to_all x0 -> x4, blocking collectives: none -> 94.9 us  [the longest x1 38.1 us: packed(): own = lax.all_to_all(mine, 'row', 0, 0, axis_index_groups=same_core)]
    scatter x2 -> x0, local copies, waits for them, and re-layouts: 76.1 us -> none  [selected(): return jnp.zeros((order_full,), jnp.float32).at[rows].set(1.0)]
    dot_general x7 -> x3, matrix products: 47.8 us -> 2.59 us  [the longest x1 1.3 us: per_device(): lax.dot_general(diag_inverse_one, right, (((0,), (0,)), ((), ())), precis...]
    pallas_call x0 -> x4, Pallas kernels: none -> 29.4 us  [the longest x1 15.9 us: packed_front_product(): pl.pallas_call(packed_front_kernel, grid=(STEPS,), out_shape=jax.ShapeDty...]
    ppermute x0 -> x4, starting transfers between devices: none -> 10.9 us  [the longest x1 4.51 us: per_device(): got = lax.ppermute(sent, ('row', 'col'), turn)]
  transfers between devices with their start and end apart: 6 -> 4, of which waited for: 6 -> 3; matrix products, arithmetic and copies ran while one was open for 4% -> 4% of each run, Pallas kernels for 0% -> 8%
where the time goes in v1:
time: 152 us; the launch traced here: 151 us
  blocking collectives  94.9 us (62%)
  Pallas kernels  29.4 us (19%)
  starting transfers between devices  10.9 us (7%)
  local copies, waits for them, and re-layouts  5.66 us (4%)
  waiting for transfers between devices  4.1 us (3%)
  matrix products  2.59 us (2%)
  other arithmetic  2.07 us (1%)
  between operations  1.52 us (1%)
    all_to_all x1, blocking collectives, packed(): own = lax.all_to_all(mine, 'row', 0, 0, axis_index_groups=same_core)  38.1 us
    all_to_all x1, blocking collectives, packed(): lax.all_to_all(parts, 'col', 0, 0)  35.8 us
    all_to_all x2, blocking collectives, spread(): lax.all_to_all(jnp.broadcast_to(x, (copies,) + x.shape), axis, 0, 0, axis...  21 us
    pallas_call x1, Pallas kernels, packed_front_product(): pl.pallas_call(packed_front_kernel, grid=(STEPS,), out_shape=jax.ShapeDty...  15.9 us
    pallas_call x1, Pallas kernels, local_solved(): pl.pallas_call(local_kernel, out_shape=[jax.ShapeDtypeStruct((2, sn, bloc...  12.7 us
    ppermute x1, starting transfers between devices, per_device(): got = lax.ppermute(sent, ('row', 'col'), turn)  4.51 us
    unnamed x18, local copies, waits for them, and re-layouts  3.61 us
  transfers between devices with their start and end apart: 4, of which 3 were waited for; matrix products, arithmetic and copies ran while one was open for 4% of the time, Pallas kernels for 8%

profile of v1, /device:TPU:1, one launch (start us, length us, event | category | flops | bytes accessed | tf_op | source)
XLA Modules:
  0.0 151.5 jit_solution(18089960022258944950)
XLA Ops:
  0.7 1.0 constant_dynamic-slice_fusion.1
  1.6 4.5 %collective-permute-start.2 = (f32[96,512]{1,0:T(8,128)S(1)}, f32[96,512]{1,0:T(8,128)S(1)}, u32[]{:S(2)}, u32[]{:S(2)}) collective-permute-start(f32[96,512]{1,0:T(8,128)S(1)} %pad_maximum_fusion.1), channel_id=1, source_target_pairs={{0,0},{1,16},{2,32},{3,48},{4,64},{5,80},{6,96},{7,112},{8,128},{9... | collective-permute-start | bytes 589832 | tf_op jit(solution)/shard_map/ppermute | solution.py:336
  6.2 1.8 %copy.28 = f32[256,256]{0,1:T(8,128)} copy(f32[256,256]{1,0:T(8,128)} %param.14) | data formatting | bytes 524288 | tf_op args[3]
  8.0 1.8 %copy.29 = f32[256,256]{0,1:T(8,128)} copy(f32[256,256]{1,0:T(8,128)} %param.15) | data formatting | bytes 524288 | tf_op args[4]
  9.7 0.6 pad_add_fusion.place
  10.4 0.0 copy-start.1
  10.4 0.0 copy-start.2
  10.4 0.0 copy-start.8
  10.4 0.0 copy-start.9
  10.4 12.7 %shard_map.120 = (bf16[2,256,1536]{2,1,0:T(8,128)(2,1)S(1)}, bf16[2,256,1536]{2,1,0:T(8,128)(2,1)}, f32[2,2,16,96]{3,2,1,0:T(8,128)S(1)}, f32[2,2,96,16]{3,2,1,0:T(8,128)S(1)}, f32[16,16]{1,0:T(8,128)}) custom-call(s32[2]{0:T(128)} %pad_add_fusion.place, s32[1,12288]{1,0:T(1,128)} %bitcast.37, s32[1,8192]{1,0:T(1,128)} %bitcast.38, f32[1536,256]{1,0:T(8,128)} %panel_one.1, ...), custom_call_target="tpu_custom_call" | custom-call | flops 6000000000 | bytes 8000000 | tf_op jit(solution)/shard_map/pallas_call | solution.py:79
  23.1 1.3 reduce_max.9
  25.1 0.0 collective-permute-done.2
  25.1 0.0 copy-done.1
  25.1 0.0 copy-done.2
  25.1 0.0 copy-done.8
  25.1 0.0 copy-done.9
  25.1 95.8 %conditional.1 = (f32[96,256]{1,0:T(8,128)S(1)}, f32[96,256]{1,0:T(8,128)S(1)}, f32[2,16,256]{2,0,1:T(2,128)S(1)}) conditional(s32[]{:T(128)} %convert_element_type.35, (s32[12288]{0:T(1024)S(1)}, s32[]{:T(128)}, s32[]{:T(128)}, s32[]{:T(128)}, f32[96,512]{1,0:T(8,128)S(1)}, /*index=5*/f32[256,256]{1,0:T(8,128)S(1)}, s32[8192]{0:T(1024)S(1)}, ...), branch_computations={%region_1.7_spmd, %region_7.8_spmd} | conditional | flops 7547757568 | bytes 66914268 | solution.py:372
  25.4 0.0 copy-start.13
  25.4 0.5 branch_1_fun.3
  25.9 38.1 %all_to_all.27.own = f32[8,112,256]{2,1,0:T(8,128)S(1)} all-to-all(f32[8,112,256]{2,1,0:T(8,128)S(1)} %branch_1_fun.3), channel_id=1, replica_groups={{0,32,64,96,128,160,192,224},{16,48,80,112,144,176,208,240},{1,33,65,97..., dimensions={0} | all-to-all | bytes 1835008 | tf_op jit(solution)/shard_map/cond/branch_1_fun/all_to_all | solution.py:344
  64.0 0.0 copy-start.4
  64.0 1.8 %collective-permute-start = (f32[8,112,256]{2,1,0:T(8,128)S(1)}, f32[8,112,256]{2,1,0:T(8,128)S(1)}, u32[]{:S(2)}, u32[]{:S(2)}) collective-permute-start(f32[8,112,256]{2,1,0:T(8,128)S(1)} %all_to_all.27.own), channel_id=1, source_target_pairs={{0,16},{16,0},{32,48},{48,32},{64,80},{80,64},{96,112},{112,96},{1... | collective-permute-start | bytes 2752520 | tf_op jit(solution)/shard_map/cond/branch_1_fun/ppermute | solution.py:345
  65.8 2.1 %collective-permute-done.other = f32[8,112,256]{2,1,0:T(8,128)S(1)} collective-permute-done((f32[8,112,256]{2,1,0:T(8,128)S(1)}, f32[8,112,256]{2,1,0:T(8,128)S(1)}, u32[]{:S(2)}, u32[]{:S(2)}) %collective-permute-start) | collective-permute-done | bytes 917536 | tf_op jit(solution)/shard_map/cond/branch_1_fun/ppermute | solution.py:345
  67.9 0.0 copy-start.11
  67.9 0.0 copy-done.4
  67.9 1.0 copy-done.11
  68.8 0.0 copy-done.13
  68.9 15.9 %branch_1_fun.4 = f32[16,144,256]{2,1,0:T(8,128)} custom-call(s32[1]{0:T(128)} %bitcast.4.core, f32[1536,1536]{1,0:T(8,128)} %get-tuple-element.82.front, f32[8,112,256]{2,1,0:T(8,128)} %copy-done.4, f32[8,112,256]{2,1,0:T(8,128)} %copy-done.11, f32[2,2,96,16]{3,2,1,0:T(8,128)S(1)} %get-tuple-element.91.slots_t, ...), custom_call_target="tpu_custom_call" | custom-call | flops 7247757312 | bytes 20000000 | tf_op jit(solution)/shard_map/cond/branch_1_fun/pallas_call | solution.py:188
  84.8 35.8 %all_to_all.28.parts = f32[16,144,256]{2,1,0:T(8,128)S(1)} all-to-all(f32[16,144,256]{2,1,0:T(8,128)} %branch_1_fun.4), channel_id=1, replica_groups=mesh['row'=16,'col'=16] {'col'}, dimensions={0} | all-to-all | bytes 4718592 | tf_op jit(solution)/shard_map/cond/branch_1_fun/all_to_all | solution.py:348
  120.6 0.3 branch_1_fun.5
  120.9 0.0 copy-start.7
  121.0 0.0 copy-start.5
  121.0 1.6 %collective-permute-start.3 = (f32[2,8,256]{2,0,1:T(2,128)S(1)}, f32[2,8,256]{2,0,1:T(2,128)S(1)}, u32[]{:S(2)}, u32[]{:S(2)}) collective-permute-start(f32[2,8,256]{2,0,1:T(2,128)S(1)} %constant_dynamic-slice_fusion), channel_id=1, source_target_pairs={{0,16},{16,0},{32,48},{48,32},{64,80},{80,64},{96,112},{112,96},{1... | collective-permute-start | bytes 49160 | tf_op jit(solution)/shard_map/ppermute | solution.py:379
  122.5 0.8 collective-permute-done.3
  123.4 10.8 %all_to_all.29 = f32[8,2,8,256]{3,2,1,0:T(8,128)S(1)} all-to-all(f32[8,2,8,256]{3,2,1,0:T(8,128)S(1)} %broadcast_in_dim.37), channel_id=1, replica_groups={{0,32,64,96,128,160,192,224},{16,48,80,112,144,176,208,240},{1,33,65,97..., dimensions={0} | all-to-all | bytes 262144 | tf_op jit(solution)/shard_map/all_to_all | solution.py:331
  134.3 10.2 %all_to_all.30 = f32[16,2,8,256]{3,2,1,0:T(8,128)S(1)} all-to-all(f32[16,2,8,256]{3,2,1,0:T(8,128)S(1)} %broadcast_in_dim.38), channel_id=1, replica_groups=mesh['row'=16,'col'=16] {'col'}, dimensions={0} | all-to-all | bytes 524288 | tf_op jit(solution)/shard_map/all_to_all | solution.py:331
  144.5 0.0 copy-start.6
  144.5 3.0 %collective-permute-start.4 = (f32[16,2,8,256]{3,2,0,1:T(8,128)S(1)}, f32[16,2,8,256]{3,2,0,1:T(8,128)S(1)}, u32[]{:S(2)}, u32[]{:S(2)}) collective-permute-start(f32[16,2,8,256]{3,2,0,1:T(8,128)S(1)} %copy.35), channel_id=1, source_target_pairs={{0,16},{16,0},{32,48},{48,32},{64,80},{80,64},{96,112},{112,96},{1... | collective-permute-start | bytes 786440 | tf_op jit(solution)/shard_map/ppermute | solution.py:382
  147.6 1.2 collective-permute-done.4
  148.8 0.0 copy-done.5
  148.9 0.0 copy-done.7
  148.9 0.0 copy-start
  148.9 0.4 fusion.10
  149.3 0.9 convolution_negate_fusion
  150.2 0.0 copy-done.6
  150.2 1.3 convolution_add_fusion
  151.5 0.0 copy-done
  (12 shorter events, 0.2 us)
Async XLA Ops:
  1.6 23.4 %collective-permute-start.2 = (f32[96,512]{1,0:T(8,128)S(1)}, f32[96,512]{1,0:T(8,128)S(1)}, u32[]{:S(2)}, u32[]{:S(2)}) collective-permute-start(f32[96,512]{1,0:T(8,128)S(1)} %pad_maximum_fusion.1), channel_id=1, source_target_pairs={{0,0},{1,16},{2,32},{3,48},{4,64},{5,80},{6,96},{7,112},{8,128},{9... | collective-permute-start | bytes 589832 | tf_op jit(solution)/shard_map/ppermute | solution.py:336
  10.4 14.7 %copy-start.1 = (f32[256,256]{1,0:T(8,128)S(1)}, f32[256,256]{1,0:T(8,128)}, u32[]{:S(2)}) copy-start(f32[256,256]{1,0:T(8,128)} %param.14) | copy-start | bytes 786436
  10.4 14.7 %copy-start.2 = (f32[256,256]{1,0:T(8,128)S(1)}, f32[256,256]{1,0:T(8,128)}, u32[]{:S(2)}) copy-start(f32[256,256]{1,0:T(8,128)} %param.15) | copy-start | bytes 786436
  10.4 14.7 %copy-start.8 = (s32[12288]{0:T(1024)S(1)}, s32[12288]{0:T(1024)}, u32[]{:S(2)}) copy-start(s32[12288]{0:T(1024)} %param.18) | copy-start | bytes 147460
  10.4 14.7 %copy-start.9 = (s32[8192]{0:T(1024)S(1)}, s32[8192]{0:T(1024)}, u32[]{:S(2)}) copy-start(s32[8192]{0:T(1024)} %param.19) | copy-start | bytes 98308
  25.4 43.5 %copy-start.13 = (bf16[2,256,1536]{2,1,0:T(8,128)(2,1)S(1)}, bf16[2,256,1536]{2,1,0:T(8,128)(2,1)}, u32[]{:S(2)}) copy-start(bf16[2,256,1536]{2,1,0:T(8,128)(2,1)} %get-tuple-element.93.st_lo) | copy-start | bytes 4718596 | tf_op jit(solution)/shard_map/cond
  64.0 3.9 %copy-start.4 = (f32[8,112,256]{2,1,0:T(8,128)}, f32[8,112,256]{2,1,0:T(8,128)S(1)}, u32[]{:S(2)}) copy-start(f32[8,112,256]{2,1,0:T(8,128)S(1)} %all_to_all.27.own) | copy-start | bytes 2752516 | tf_op jit(solution)/shard_map/cond
  64.0 3.9 %collective-permute-start = (f32[8,112,256]{2,1,0:T(8,128)S(1)}, f32[8,112,256]{2,1,0:T(8,128)S(1)}, u32[]{:S(2)}, u32[]{:S(2)}) collective-permute-start(f32[8,112,256]{2,1,0:T(8,128)S(1)} %all_to_all.27.own), channel_id=1, source_target_pairs={{0,16},{16,0},{32,48},{48,32},{64,80},{80,64},{96,112},{112,96},{1... | collective-permute-start | bytes 2752520 | tf_op jit(solution)/shard_map/cond/branch_1_fun/ppermute | solution.py:345
  67.9 1.0 copy-start.11
  120.9 27.9 %copy-start.7 = (f32[96,256]{1,0:T(8,128)}, f32[96,256]{1,0:T(8,128)S(1)}, u32[]{:S(2)}) copy-start(f32[96,256]{1,0:T(8,128)S(1)} %get-tuple-element.105) | copy-start | bytes 294916
  121.0 27.9 %copy-start.5 = (f32[256,256]{1,0:T(8,128)S(1)}, f32[256,256]{1,0:T(8,128)}, u32[]{:S(2)}) copy-start(f32[256,256]{1,0:T(8,128)} %param.16) | copy-start | bytes 786436
  121.0 2.4 %collective-permute-start.3 = (f32[2,8,256]{2,0,1:T(2,128)S(1)}, f32[2,8,256]{2,0,1:T(2,128)S(1)}, u32[]{:S(2)}, u32[]{:S(2)}) collective-permute-start(f32[2,8,256]{2,0,1:T(2,128)S(1)} %constant_dynamic-slice_fusion), channel_id=1, source_target_pairs={{0,16},{16,0},{32,48},{48,32},{64,80},{80,64},{96,112},{112,96},{1... | collective-permute-start | bytes 49160 | tf_op jit(solution)/shard_map/ppermute | solution.py:379
  144.5 5.7 %copy-start.6 = (f32[256,256]{1,0:T(8,128)S(1)}, f32[256,256]{1,0:T(8,128)}, u32[]{:S(2)}) copy-start(f32[256,256]{1,0:T(8,128)} %param.17) | copy-start | bytes 786436
  144.5 4.2 %collective-permute-start.4 = (f32[16,2,8,256]{3,2,0,1:T(8,128)S(1)}, f32[16,2,8,256]{3,2,0,1:T(8,128)S(1)}, u32[]{:S(2)}, u32[]{:S(2)}) collective-permute-start(f32[16,2,8,256]{3,2,0,1:T(8,128)S(1)} %copy.35), channel_id=1, source_target_pairs={{0,16},{16,0},{32,48},{48,32},{64,80},{80,64},{96,112},{112,96},{1... | collective-permute-start | bytes 786440 | tf_op jit(solution)/shard_map/ppermute | solution.py:382
  148.9 2.6 %copy-start = (f32[256,256]{1,0:T(8,128)}, f32[256,256]{1,0:T(8,128)S(1)}, u32[]{:S(2)}) copy-start(f32[256,256]{1,0:T(8,128)S(1)} %bitcast_add_fusion) | copy-start | bytes 786436

commit v2 on v1

v2 whole, which is shorter than its diff:
```python
import functools

import jax
import jax.numpy as jnp
from jax import lax
from jax.experimental import pallas as pl
from jax.experimental.pallas import tpu as pltpu
from jax.sharding import PartitionSpec as P

HIGHEST = lax.Precision.HIGHEST
F32 = jnp.float32
BF16 = jnp.bfloat16
NT = (((1,), (1,)), ((), ()))
NN = (((1,), (0,)), ((), ()))
STEPS = 2
PIECE = 96
SLOTS = 112
PAIR = 2 * PIECE
WIDE = 256
WINDOW = 16 * PIECE + 128


def split(x):
    hi = x.astype(BF16)
    return hi, (x - hi.astype(F32)).astype(BF16)


def dot3(left, right, dims=NN):
    (lh, ll), (rh, rl) = left, right
    dot = functools.partial(lax.dot_general, dimension_numbers=dims, preferred_element_type=F32)
    return dot(lh, rh) + (dot(lh, rl) + dot(ll, rh))


def matmul(left, right):
    return jnp.dot(left, right, precision=HIGHEST, preferred_element_type=F32)


def one_hot(values, count):
    return jnp.where(values == lax.broadcasted_iota(jnp.int32, (count, values.shape[1]), 0), 1.0, 0.0).astype(BF16)


def one_dot(left, right, dims=NN):
    return lax.dot_general(left, right, dims, preferred_element_type=F32)


def tables_kernel(place, rows_one, rows_two, slots, slots_t, counts):
    row_at = lax.broadcasted_iota(jnp.int32, (PAIR, PAIR), 0)
    col_at = lax.broadcasted_iota(jnp.int32, (PAIR, PAIR), 1)
    near = (row_at >= PIECE) == (col_at >= PIECE)
    together = jnp.where(near, 1.0, 0.0).astype(BF16)
    earlier = jnp.where(near & (row_at < col_at), 1.0, 0.0).astype(BF16)
    same = jnp.where(row_at == col_at, 1.0, 0.0).astype(BF16)
    before = jnp.where(lax.broadcasted_iota(jnp.int32, (16, PAIR), 1) >= PIECE, float(SLOTS), 0.0)
    length = 0.0
    slots[...] = jnp.full(slots.shape, -1.0, F32)
    for at, rows in enumerate((rows_one, rows_two)):
        index = rows[...]
        piece = piece_of(index)
        length = length + one_dot(
            one_hot(lax.shift_right_logical(piece, 4), 16), one_hot(lax.bitwise_and(piece, 15), 16), NT
        )
        marks = []
        for which in range(2):
            first = jnp.sum(jnp.where(index < 16 * PIECE * place[which], 1.0, 0.0)).astype(jnp.int32)
            first = jnp.minimum(first // 128 * 128, index.shape[1] - WINDOW)
            some = rows[:, pl.ds(pl.multiple_of(first, 128), WINDOW)]
            pair = lax.shift_right_logical(piece_of(some), 1)
            inner = jnp.where(lax.shift_right_logical(pair, 3) == place[which], lax.bitwise_and(pair, 7), -1)
            marks.append(one_dot(one_hot(inner, 16), one_hot(some - PAIR * pair, PAIR), NT)[:8])
        marks = jnp.concatenate(marks, axis=0)
        marks_low = marks.astype(BF16)
        slot = jnp.where(marks > 0.5, one_dot(marks_low, earlier) + before, -1.0)
        before = before + one_dot(marks_low, together)
        slots[:, WIDE * at:WIDE * at + PAIR] = slot
        slots_t[at] = one_dot(same, slot.astype(BF16), NT)
    counts[...] = length


def piece_of(index):
    return lax.shift_right_logical(lax.shift_right_logical(index, 5) * 43691, 17)


def list_tables(place, rows_one, rows_two):
    vmem = pl.BlockSpec(memory_space=pltpu.VMEM)
    return pl.pallas_call(
        tables_kernel,
        out_shape=[
            jax.ShapeDtypeStruct((16, 2 * WIDE), F32),
            jax.ShapeDtypeStruct((2, PAIR, 16), F32),
            jax.ShapeDtypeStruct((16, 16), F32),
        ],
        in_specs=[pl.BlockSpec(memory_space=pltpu.SMEM)] + [vmem] * 2,
        out_specs=[vmem] * 3,
        compiler_params=pltpu.CompilerParams(vmem_limit_bytes=24 << 20),
        cost_estimate=pl.CostEstimate(flops=200_000_000, bytes_accessed=300_000, transcendentals=0),
    )(place, rows_one[None, :], rows_two[None, :])


def local_kernel(slots_t, panel_one, panel_two, lower_one, lower_two, hi, lo):
    for at, (panel, lower) in enumerate(((panel_one, lower_one), (panel_two, lower_two))):
        marks = jnp.where(slots_t[at] >= 0.0, 1.0, 0.0)
        chosen = [panel[PAIR * q:PAIR * q + PAIR, :] * marks[:, q:q + 1] for q in range(8)]
        hi[at], lo[at] = split(dot3(split(lower[...].T), split(jnp.concatenate(chosen, axis=0)), NT))


def local_solved(slots_t, panel_one, panel_two, lower_one, lower_two):
    block, sn = panel_one.shape
    vmem = pl.BlockSpec(memory_space=pltpu.VMEM)
    return pl.pallas_call(
        local_kernel,
        out_shape=[jax.ShapeDtypeStruct((2, sn, block), BF16)] * 2,
        in_specs=[vmem] * 5,
        out_specs=[vmem] * 2,
        compiler_params=pltpu.CompilerParams(vmem_limit_bytes=24 << 20),
        cost_estimate=pl.CostEstimate(flops=2_000_000_000, bytes_accessed=6_000_000, transcendentals=0),
    )(slots_t, panel_one, panel_two, lower_one, lower_two)


def chosen_rows(slot, first, count):
    wanted = (first + lax.broadcasted_iota(jnp.int32, (count, slot.shape[1]), 0)).astype(F32)
    return jnp.where(slot == wanted, 1.0, 0.0).astype(BF16)


def place_rows(slot, count):
    wanted = lax.broadcasted_iota(jnp.int32, (slot.shape[0], count), 1).astype(F32)
    return jnp.where(slot == wanted, 1.0, 0.0).astype(BF16)


def pack(chosen, block_one, block_two):
    gap = jnp.zeros((WIDE - PAIR, block_one.shape[1]), BF16)
    parts = zip(split(block_one), split(block_two))
    hi, lo = [jnp.concatenate([one, gap, two, gap], axis=0) for one, two in parts]
    return one_dot(chosen, hi) + one_dot(chosen, lo)


def piece_kernel(place, panel_one, panel_two, slots, lower_one, lower_two, out):
    at = place[1] % 2 * 8 + place[1] // 2
    rows = pl.ds(pl.multiple_of(at * PIECE, PIECE), PIECE)
    one = dot3(split(panel_one[rows, :]), split(lower_one[...]))
    two = dot3(split(panel_two[rows, :]), split(lower_two[...]))
    chosen = chosen_rows(slots[pl.ds(at // 2, 1), :], at % 2 * SLOTS, SLOTS)
    out[...] = pack(chosen, jnp.concatenate([one, one], axis=0), jnp.concatenate([two, two], axis=0))


def packed_piece(place, panel_one, panel_two, slots, lower_one, lower_two):
    vmem = pl.BlockSpec(memory_space=pltpu.VMEM)
    return pl.pallas_call(
        piece_kernel,
        out_shape=jax.ShapeDtypeStruct((SLOTS, lower_one.shape[0]), F32),
        in_specs=[pl.BlockSpec(memory_space=pltpu.SMEM)] + [vmem] * 5,
        out_specs=vmem,
        compiler_params=pltpu.CompilerParams(vmem_limit_bytes=16 << 20),
        cost_estimate=pl.CostEstimate(flops=200_000_000, bytes_accessed=2_000_000, transcendentals=0),
    )(place, panel_one, panel_two, slots, lower_one, lower_two)


def packed_front_kernel(
    place, front, own, other, slots_t, slots, st_hi, st_lo, out, give, tiles, s_hi, s_lo, diag, arrived
):
    core = place[0] % 2
    copies = [
        pltpu.make_async_copy(front.at[pl.ds(step * tiles.shape[1], tiles.shape[1]), :], tiles.at[step], arrived.at[step])
        for step in range(STEPS)
    ]
    for copy in copies:
        copy.start()
    half = s_hi.shape[0] // 2
    sn = st_hi.shape[1]
    tile = tiles.shape[1]
    pairs = tile // PAIR

    for at, ref in enumerate((own, other)):
        whose = core if at == 0 else 1 - core
        slot = [jnp.where(whose == 0, slots_t[which, :, 8:12], slots_t[which, :, 12:16]) for which in range(2)]
        for q in range(4):
            spot = [place_rows(slot[which][:, q:q + 1], 2 * SLOTS) for which in range(2)]
            parts = jnp.concatenate(split(ref[2 * q:2 * q + 2].reshape(2 * SLOTS, sn)), axis=1)
            rows = one_dot(jnp.concatenate(spot, axis=0), parts).astype(BF16)
            into = pl.ds(pl.multiple_of(whose * half + PAIR * q, PAIR), PAIR)
            for which in range(2):
                s_hi[into, sn * which:sn * which + sn] = rows[PAIR * which:PAIR * which + PAIR, :sn]
                s_lo[into, sn * which:sn * which + sn] = rows[PAIR * which:PAIR * which + PAIR, sn:]
    diag[...] = jnp.zeros_like(diag)

    for step in range(STEPS):
        begin = tile * step
        copies[step].wait()
        total = dot3(split(tiles[step]), (s_hi[...], s_lo[...]))
        for q in range(pairs):
            now = pairs * step + q
            rows = slice(PAIR * q, PAIR * q + PAIR)
            chosen = chosen_rows(slots[pl.ds(now, 1), :], 0, 2 * SLOTS)
            packed = pack(chosen, total[rows, :sn], total[rows, sn:])
            out[pl.ds(2 * now, 2), :SLOTS, :] = packed.reshape(2, SLOTS, sn)
        for at in range(2):
            left = st_hi[at, :, pl.ds(begin, tile)], st_lo[at, :, pl.ds(begin, tile)]
            diag[at] += dot3(left, split(total[:, sn * at:sn * at + sn]))

    share = give.shape[1] // 2
    for ref, begin, whose in ((out, SLOTS, core), (give, 0, 1 - core)):
        for d in range(out.shape[0]):
            rows = pl.ds(pl.multiple_of((2 * d + whose) * share, share), share)
            for at in range(2):
                ref[d, begin + share * at:begin + share * at + share, :] = diag[at, rows, :]


def packed_front_product(place, front, own, other, slots_t, slots, st_hi, st_lo, col_count):
    rows, cols = front.shape
    sn = own.shape[2]
    share = sn // col_count
    vmem = pl.BlockSpec(memory_space=pltpu.VMEM)
    return pl.pallas_call(
        packed_front_kernel,
        out_shape=[
            jax.ShapeDtypeStruct((col_count, SLOTS + share, sn), F32),
            jax.ShapeDtypeStruct((col_count, share, sn), F32),
        ],
        in_specs=[pl.BlockSpec(memory_space=pltpu.SMEM), pl.BlockSpec(memory_space=pl.ANY)] + [vmem] * 6,
        out_specs=[vmem] * 2,
        scratch_shapes=[
            pltpu.VMEM((STEPS, rows // STEPS, cols), F32),
            pltpu.VMEM((cols, 2 * sn), BF16),
            pltpu.VMEM((cols, 2 * sn), BF16),
            pltpu.VMEM((2, sn, sn), F32),
            pltpu.SemaphoreType.DMA((STEPS,)),
        ],
        compiler_params=pltpu.CompilerParams(vmem_limit_bytes=40 << 20),
        cost_estimate=pl.CostEstimate(flops=12 * rows * cols * sn, bytes_accessed=20_000_000, transcendentals=0),
    )(place, front, own, other, slots_t, slots, st_hi, st_lo)


def sum_kernel(place, parts, slots_t, inverse_one, product_two, shares):
    total = parts[0]
    for d in range(1, parts.shape[0]):
        total = total + parts[d]
    shares[...] = total[SLOTS:, :]
    total = total[:SLOTS, :]
    hi = total.astype(BF16)
    mid, low = split(total - hi.astype(F32))
    for which in range(2):
        slot = slots_t[which]
        picked = lax.broadcasted_iota(jnp.int32, slot.shape, 1) == place[1] // 2
        slot = jnp.sum(jnp.where(picked, slot, 0.0), axis=1, keepdims=True)
        slot = jnp.where(place[1] % 2 == 0, slot[:PIECE], slot[PIECE:] - float(SLOTS))
        spot = place_rows(slot, SLOTS)
        rows = one_dot(spot, hi) + (one_dot(spot, mid) + one_dot(spot, low))
        if which == 0:
            inverse_one[...] = -rows
        else:
            product_two[...] = rows


def summed_piece(place, parts, slots_t):
    sn = parts.shape[2]
    vmem = pl.BlockSpec(memory_space=pltpu.VMEM)
    return pl.pallas_call(
        sum_kernel,
        out_shape=[jax.ShapeDtypeStruct((PIECE, sn), F32)] * 2
        + [jax.ShapeDtypeStruct((parts.shape[1] - SLOTS, sn), F32)],
        in_specs=[pl.BlockSpec(memory_space=pltpu.SMEM), vmem, vmem],
        out_specs=[vmem] * 3,
        compiler_params=pltpu.CompilerParams(vmem_limit_bytes=48 << 20),
        cost_estimate=pl.CostEstimate(flops=100_000_000, bytes_accessed=3_000_000, transcendentals=0),
    )(place, parts, slots_t)


def finish_kernel(place, near, far, pivot_one, pivot_two, product_two, inverse_one, panel_two, inverse_two, sums):
    share = near.shape[2]
    for ref, whose in ((near, place[0] % 2), (far, 1 - place[0] % 2)):
        for d in range(near.shape[0]):
            for at in range(2):
                sums[at, pl.ds(pl.multiple_of((2 * d + whose) * share, share), share), :] = ref[d, at]
    first = pivot_one[...] + sums[0]
    inverse_one[...] = first
    panel_two[...] = -matmul(product_two[...], first)
    inverse_two[...] = pivot_two[...] + matmul(first.T, matmul(sums[1], first))


def finish(place, near, far, pivot_one, pivot_two, product_two):
    square = jax.ShapeDtypeStruct(pivot_one.shape, F32)
    vmem = pl.BlockSpec(memory_space=pltpu.VMEM)
    return pl.pallas_call(
        finish_kernel,
        out_shape=[square, jax.ShapeDtypeStruct(product_two.shape, F32), square],
        in_specs=[pl.BlockSpec(memory_space=pltpu.SMEM)] + [vmem] * 5,
        out_specs=[vmem] * 3,
        scratch_shapes=[pltpu.VMEM((2,) + pivot_one.shape, F32)],
        compiler_params=pltpu.CompilerParams(vmem_limit_bytes=16 << 20),
        cost_estimate=pl.CostEstimate(flops=600_000_000, bytes_accessed=2_000_000, transcendentals=0),
    )(place, near, far, pivot_one, pivot_two, product_two)


def front_kernel(core, front, own, other, st_hi, st_lo, out, s_hi, s_lo, diag):
    step = pl.program_id(0)
    half = own.shape[0]
    sn = st_hi.shape[1]
    tile = front.shape[0]
    pieces = tile // 96

    @pl.when(step == 0)
    def _():
        for at, ref in enumerate((own, other)):
            h, l = split(ref[...])
            s_hi[at] = h
            s_lo[at] = l
        diag[...] = jnp.zeros_like(diag)

    total = None
    for at in range(2):
        which = core[0] if at == 0 else 1 - core[0]
        columns = pl.ds(pl.multiple_of(which * half, half), half)
        part = dot3(split(front[:, columns]), (s_hi[at], s_lo[at]))
        total = part if total is None else total + part
    for p in range(pieces):
        out[pieces * step + p, :96, :] = total[96 * p:96 * p + 96, :]
    for at in range(2):
        cols = slice(sn * at, sn * at + sn)
        diag[:, cols] += dot3((st_hi[at], st_lo[at]), split(total[:, cols]))

    @pl.when(step == STEPS - 1)
    def _():
        share = sn // out.shape[0]
        for d in range(out.shape[0]):
            out[d, 96:, :] = diag[share * d:share * d + share, :]


def front_product(core, front, own, other, st_hi, st_lo, col_count):
    rows, cols = front.shape
    wide = own.shape[1]
    sn = wide // 2
    tile = rows // STEPS
    whole = lambda a: pl.BlockSpec(a.shape, lambda i: (0,) * a.ndim)
    out = (col_count, rows // col_count + sn // col_count, wide)
    return pl.pallas_call(
        front_kernel,
        grid=(STEPS,),
        out_shape=jax.ShapeDtypeStruct(out, F32),
        in_specs=[
            pl.BlockSpec(memory_space=pltpu.SMEM),
            pl.BlockSpec((tile, cols), lambda i: (i, 0)),
            whole(own), whole(other),
            pl.BlockSpec((2, sn, tile), lambda i: (0, 0, i)),
            pl.BlockSpec((2, sn, tile), lambda i: (0, 0, i)),
        ],
        out_specs=pl.BlockSpec(out, lambda i: (0, 0, 0)),
        scratch_shapes=[
            pltpu.VMEM((2, cols // 2, wide), BF16),
            pltpu.VMEM((2, cols // 2, wide), BF16),
            pltpu.VMEM((sn, wide), F32),
        ],
        compiler_params=pltpu.CompilerParams(vmem_limit_bytes=56 << 20),
        cost_estimate=pl.CostEstimate(flops=6 * rows * cols * wide, bytes_accessed=20_000_000, transcendentals=0),
    )(core, front, own, other, st_hi, st_lo)


def marked(rows, first, count):
    wanted = first + lax.broadcasted_iota(jnp.int32, (count, 1), 0)
    return jnp.any(rows[None, :] == wanted, axis=1, keepdims=True).astype(F32)


def per_device(
    front, panel_one, panel_two, lower_one, lower_two, pivot_one, pivot_two, rows_one, rows_two
):
    n = lax.axis_size("row")
    row = lax.axis_index("row")
    col = lax.axis_index("col")
    block, sn = panel_one.shape
    piece = block // n
    half = n // 2
    core = row % 2
    parities = [list(range(0, n, 2)), list(range(1, n, 2))]
    swap = [(r, r ^ 1) for r in range(n)]

    def exchange(x, axis, groups=None):
        return lax.all_to_all(x, axis, 0, 0, axis_index_groups=groups)

    def spread(x, axis, copies, groups=None):
        return exchange(jnp.broadcast_to(x, (copies,) + x.shape), axis, groups)

    turn = [(r * n + c, c * n + r) for r in range(n) for c in range(n)]
    place = jnp.stack([row, col])
    slots, slots_t, counts = list_tables(place, rows_one, rows_two)

    def complete(keep, product_two):
        keep = jnp.sum(spread(keep, "row", half, parities), axis=0)
        near = spread(keep, "col", n)
        return finish(place, near, lax.ppermute(near, "row", swap), pivot_one, pivot_two, product_two)

    def packed(place, front, slots, slots_t):
        mine = packed_piece(place, panel_one, panel_two, slots, lower_one, lower_two)
        mine = lax.ppermute(mine, ("row", "col"), turn)
        st_hi, st_lo = local_solved(slots_t, panel_one, panel_two, lower_one, lower_two)
        own = spread(mine, "row", half, parities)
        other = lax.ppermute(own, "row", swap)
        parts, give = packed_front_product(place, front, own, other, slots_t, slots, st_hi, st_lo, n)
        shares = parts[:, SLOTS:] + lax.ppermute(give, "row", swap)
        parts = exchange(lax.dynamic_update_slice(parts, shares, (0, SLOTS, 0)), "col")
        inverse_one, product_two, keep = summed_piece(place, parts, slots_t)
        return inverse_one, *complete(keep.reshape(2, sn // n // 2, sn), product_two)

    def dense(place, front, slots, slots_t):
        at = (col % 2 * half + col // 2) * piece
        solved = jnp.concatenate(
            [
                matmul(marked(rows, row * block + at, piece) * lax.dynamic_slice_in_dim(panel, at, piece, 0), lower)
                for rows, panel, lower in ((rows_one, panel_one, lower_one), (rows_two, panel_two, lower_two))
            ],
            axis=1,
        )
        solved = lax.ppermute(solved, ("row", "col"), turn)
        st_hi, st_lo = local_solved(slots_t, panel_one, panel_two, lower_one, lower_two)
        own = spread(solved, "row", half, parities).reshape(block // 2, 2 * sn)
        other = lax.ppermute(own, "row", swap)
        parts = front_product(core[None], front, own, other, st_hi, st_lo, n)
        summed = jnp.sum(exchange(parts, "col"), axis=0)
        shares = summed[piece:].reshape(2, sn // n // 2, 2, sn).transpose(0, 2, 1, 3)
        keep, give = [lax.dynamic_index_in_dim(shares, c, 0, keepdims=False) for c in (core, 1 - core)]
        keep = keep + lax.ppermute(give, "row", swap)
        mine = row * block + col * piece
        inverse_one = -(marked(rows_one, mine, piece) * summed[:piece, :sn])
        return inverse_one, *complete(keep, marked(rows_two, mine, piece) * summed[:piece, sn:])

    return lax.cond(jnp.max(counts) <= SLOTS, packed, dense, place, front, slots, slots_t)


def solution(mesh):
    in_specs = (P("row", "col"), P("row", None), P("row", None), P(), P(), P(), P(), P(), P())
    out_specs = (P(("row", "col"), None), P(), P(("row", "col"), None), P())
    return jax.shard_map(
        per_device, mesh=mesh, in_specs=in_specs, out_specs=out_specs, check_vma=False
    )
```

time: 152 us -> 145 us (0.954)
  blocking collectives: 94.9 us -> 99.9 us
  local copies, waits for them, and re-layouts: 5.66 us -> 0.86 us
  Pallas kernels: 29.4 us -> 25.6 us
  matrix products: 2.59 us -> 0 us
    pallas_call x1, Pallas kernels: 12.7 us -> 1.77 us  [local_solved(): pl.pallas_call(local_kernel, out_shape=[jax.ShapeDtypeStruct((2, sn, bloc...]
    pallas_call x2 -> x4, Pallas kernels: 16.4 us -> 22.3 us  [the longest x1 13.6 us: packed_front_product(): pl.pallas_call(packed_front_kernel, out_shape=[jax.ShapeDtypeStruct((col_...]
    all_to_all x4, blocking collectives: 94.9 us -> 99.9 us  [exchange(): return lax.all_to_all(x, axis, 0, 0, axis_index_groups=groups)]
    unnamed x18 -> x4, local copies, waits for them, and re-layouts: 3.61 us -> 0.72 us
    ppermute x3, waiting for transfers between devices: 2 us -> 4.79 us  [the longest x1 2.46 us: packed(): mine = lax.ppermute(mine, ('row', 'col'), turn)]
    dot_general x3 -> x0, matrix products: 2.59 us -> none  [the longest x1 1.3 us: per_device(): lax.dot_general(diag_inverse_one, right, (((0,), (0,)), ((), ())), precis...]
    ppermute x1, waiting for transfers between devices: 2.1 us -> 0.3 us  [packed(): other = lax.ppermute(own, 'row', swap)]
  transfers between devices with their start and end apart: 4 -> 4, of which waited for: 3 -> 4; matrix products, arithmetic and copies ran while one was open for 4% -> 0% of each run, Pallas kernels for 8% -> 1%
where the time goes in v2:
time: 145 us
  blocking collectives  99.9 us (69%)
  Pallas kernels  25.6 us (18%)
  starting transfers between devices  11 us (8%)
  waiting for transfers between devices  5.09 us (4%)
    all_to_all x4, blocking collectives, exchange(): return lax.all_to_all(x, axis, 0, 0, axis_index_groups=groups)  99.9 us
    pallas_call x1, Pallas kernels, packed_front_product(): pl.pallas_call(packed_front_kernel, out_shape=[jax.ShapeDtypeStruct((col_...  13.6 us
    ppermute x1, starting transfers between devices, packed(): mine = lax.ppermute(mine, ('row', 'col'), turn)  4.64 us
    pallas_call x1, Pallas kernels, list_tables(): pl.pallas_call(tables_kernel, out_shape=[jax.ShapeDtypeStruct((16, 2 * WI...  3.69 us
    ppermute x1, starting transfers between devices, complete(): lax.ppermute(near, 'row', swap)  3.68 us
  transfers between devices with their start and end apart: 4, of which 4 were waited for; matrix products, arithmetic and copies ran while one was open for 0% of the time, Pallas kernels for 1%

profile of v2, /device:TPU:1, one launch (start us, length us, event | category | flops | bytes accessed | tf_op | source)
XLA Modules:
  0.0 144.9 jit_solution(2278903519720415229)
XLA Ops:
  0.6 0.1 pad_add_fusion.place
  0.7 3.7 %shard_map.122 = (f32[16,512]{1,0:T(8,128)S(1)}, f32[2,192,16]{2,1,0:T(8,128)}, f32[16,16]{1,0:T(8,128)S(1)}) custom-call(s32[2]{0:T(128)S(1)} %pad_add_fusion.place, s32[1,12288]{1,0:T(1,128)} %bitcast.21, s32[1,8192]{1,0:T(1,128)} %bitcast.22), custom_call_target="tpu_custom_call" | custom-call | flops 200000000 | bytes 300000 | tf_op jit(solution)/shard_map/pallas_call | solution.py:85
  4.4 0.6 reduce_max.9
  5.7 138.5 %conditional.1 = (f32[256,256]{1,0:T(8,128)S(1)}, f32[96,256]{1,0:T(8,128)S(1)}, f32[256,256]{1,0:T(8,128)}, f32[96,256]{1,0:T(8,128)}) conditional(s32[]{:T(128)} %convert_element_type.35, (s32[12288]{0:T(1024)}, s32[]{:T(128)}, s32[]{:T(128)}, f32[1536,256]{1,0:T(8,128)}, f32[256,256]{1,0:T(8,128)}, /*index=5*/s32[8192]{0:T(1024)}, ...), branch_computations={%region_1.8_spmd, %region_8.10_spmd} | conditional | flops 10147852288 | bytes 87628472 | solution.py:423
  5.9 0.0 copy-start.5
  5.9 2.6 %branch_1_fun.5 = f32[112,256]{1,0:T(8,128)S(1)} custom-call(s32[2]{0:T(128)S(1)} %get-tuple-element.88.place, f32[1536,256]{1,0:T(8,128)} %get-tuple-element.90.panel_one, f32[1536,256]{1,0:T(8,128)} %get-tuple-element.91.panel_two, f32[16,512]{1,0:T(8,128)S(1)} %get-tuple-element.92.slots, f32[256,256]{1,0:T(8,128)} %get-tuple-element.93.lower_one, ...), custom_call_target="tpu_custom_call" | custom-call | flops 200000000 | bytes 2000000 | tf_op jit(solution)/shard_map/cond/branch_1_fun/pallas_call | solution.py:147
  8.5 0.0 copy-start.3
  8.5 0.0 copy-start.7
  8.5 0.0 copy-start.8
  8.5 0.0 copy-start.9
  8.5 4.6 %collective-permute-start = (f32[112,256]{1,0:T(8,128)S(1)}, f32[112,256]{1,0:T(8,128)S(1)}, u32[]{:S(2)}, u32[]{:S(2)}) collective-permute-start(f32[112,256]{1,0:T(8,128)S(1)} %branch_1_fun.5), channel_id=1, source_target_pairs={{0,0},{1,16},{2,32},{3,48},{4,64},{5,80},{6,96},{7,112},{8,128},{9... | collective-permute-start | bytes 344072 | tf_op jit(solution)/shard_map/cond/branch_1_fun/ppermute | solution.py:391
  13.2 2.5 %collective-permute-done = f32[112,256]{1,0:T(8,128)S(1)} collective-permute-done((f32[112,256]{1,0:T(8,128)S(1)}, f32[112,256]{1,0:T(8,128)S(1)}, u32[]{:S(2)}, u32[]{:S(2)}) %collective-permute-start) | collective-permute-done | bytes 114720 | tf_op jit(solution)/shard_map/cond/branch_1_fun/ppermute | solution.py:391
  15.6 0.1 broadcast_in_dim.12
  15.7 45.3 %all_to_all.35.own = f32[8,112,256]{2,1,0:T(8,128)S(1)} all-to-all(f32[8,112,256]{2,1,0:T(8,128)S(1)} %broadcast_in_dim.12), channel_id=1, replica_groups={{0,32,64,96,128,160,192,224},{16,48,80,112,144,176,208,240},{1,33,65,97..., dimensions={0} | all-to-all | bytes 1835008 | tf_op jit(solution)/shard_map/cond/branch_1_fun/all_to_all | solution.py:375
  61.0 2.2 %collective-permute-start.1 = (f32[8,112,256]{2,1,0:T(8,128)S(1)}, f32[8,112,256]{2,1,0:T(8,128)S(1)}, u32[]{:S(2)}, u32[]{:S(2)}) collective-permute-start(f32[8,112,256]{2,1,0:T(8,128)S(1)} %all_to_all.35.own), channel_id=1, source_target_pairs={{0,16},{16,0},{32,48},{48,32},{64,80},{80,64},{96,112},{112,96},{1... | collective-permute-start | bytes 2752520 | tf_op jit(solution)/shard_map/cond/branch_1_fun/ppermute | solution.py:394
  63.3 0.0 copy-done.5
  63.3 0.0 copy-done.3
  63.3 0.0 copy-done.7
  63.3 0.0 copy-done.8
  63.3 0.0 copy-done.9
  63.3 1.8 %branch_1_fun.6 = (bf16[2,256,1536]{2,1,0:T(8,128)(2,1)S(1)}, bf16[2,256,1536]{2,1,0:T(8,128)(2,1)S(1)}) custom-call(f32[2,192,16]{2,1,0:T(8,128)S(1)} %copy-done.9, f32[1536,256]{1,0:T(8,128)S(1)} %copy-done.3, f32[1536,256]{1,0:T(8,128)S(1)} %copy-done.5, f32[256,256]{1,0:T(8,128)S(1)} %copy-done.7, f32[256,256]{1,0:T(8,128)S(1)} %copy-done.8), custom_call_target="tpu_custom_call" | custom-call | flops 2000000000 | bytes 6000000 | tf_op jit(solution)/shard_map/cond/branch_1_fun/pallas_call | solution.py:109
  65.1 0.3 collective-permute-done.1.other
  65.4 13.6 %branch_1_fun.7 = (f32[16,128,256]{2,1,0:T(8,128)S(1)}, f32[16,16,256]{2,1,0:T(8,128)S(1)}) custom-call(s32[2]{0:T(128)S(1)} %get-tuple-element.88.place, f32[1536,1536]{1,0:T(8,128)} %get-tuple-element.89.front, f32[8,112,256]{2,1,0:T(8,128)S(1)} %all_to_all.35.own, f32[8,112,256]{2,1,0:T(8,128)S(1)} %collective-permute-done.1.other, ...), custom_call_target="tpu_custom_call" | custom-call | flops 7247757312 | bytes 20000000 | tf_op jit(solution)/shard_map/cond/branch_1_fun/pallas_call | solution.py:212
  79.0 0.5 collective-permute-start.2
  79.4 1.2 collective-permute-done.2
  80.6 0.1 add_dynamic-update-slice_fusion
  80.7 33.4 %all_to_all.36.parts = f32[16,128,256]{2,1,0:T(8,128)S(1)} all-to-all(f32[16,128,256]{2,1,0:T(8,128)S(1)} %add_dynamic-update-slice_fusion), channel_id=1, replica_groups=mesh['row'=16,'col'=16] {'col'}, dimensions={0} | all-to-all | bytes 4194304 | tf_op jit(solution)/shard_map/cond/branch_1_fun/all_to_all | solution.py:375
  114.1 0.0 copy-start.11
  114.1 0.0 copy-start.13
  114.1 1.5 %branch_1_fun.8 = (f32[96,256]{1,0:T(8,128)}, f32[96,256]{1,0:T(8,128)S(1)}, f32[16,256]{1,0:T(8,128)S(1)}) custom-call(s32[2]{0:T(128)S(1)} %get-tuple-element.88.place, f32[16,128,256]{2,1,0:T(8,128)S(1)} %all_to_all.36.parts, f32[2,192,16]{2,1,0:T(8,128)S(1)} %copy-done.9), custom_call_target="tpu_custom_call" | custom-call | flops 100000000 | bytes 3000000 | tf_op jit(solution)/shard_map/cond/branch_1_fun/pallas_call | solution.py:256
  115.6 10.3 %all_to_all.37 = f32[8,2,8,256]{3,2,1,0:T(8,128)S(1)} all-to-all(f32[8,2,8,256]{3,2,1,0:T(8,128)S(1)} %broadcast_in_dim.26), channel_id=1, replica_groups={{0,32,64,96,128,160,192,224},{16,48,80,112,144,176,208,240},{1,33,65,97..., dimensions={0} | all-to-all | bytes 262144 | tf_op jit(solution)/shard_map/cond/branch_1_fun/all_to_all | solution.py:375
  126.0 10.9 %all_to_all.38.near = f32[16,2,8,256]{3,2,1,0:T(8,128)S(1)} all-to-all(f32[16,2,8,256]{3,2,1,0:T(8,128)S(1)} %broadcast_in_dim.27), channel_id=1, replica_groups=mesh['row'=16,'col'=16] {'col'}, dimensions={0} | all-to-all | bytes 524288 | tf_op jit(solution)/shard_map/cond/branch_1_fun/all_to_all | solution.py:375
  136.8 3.7 %collective-permute-start.3 = (f32[16,2,8,256]{3,2,1,0:T(8,128)S(1)}, f32[16,2,8,256]{3,2,1,0:T(8,128)S(1)}, u32[]{:S(2)}, u32[]{:S(2)}) collective-permute-start(f32[16,2,8,256]{3,2,1,0:T(8,128)S(1)} %all_to_all.38.near), channel_id=1, source_target_pairs={{0,16},{16,0},{32,48},{48,32},{64,80},{80,64},{96,112},{112,96},{1... | collective-permute-start | bytes 786440 | tf_op jit(solution)/shard_map/cond/branch_1_fun/ppermute | solution.py:387
  140.5 1.2 collective-permute-done.3.far
  141.7 0.0 copy-done.11
  141.7 0.0 copy-done.13
  141.7 2.4 %branch_1_fun.9 = (f32[256,256]{1,0:T(8,128)S(1)}, f32[96,256]{1,0:T(8,128)S(1)}, f32[256,256]{1,0:T(8,128)}) custom-call(s32[2]{0:T(128)S(1)} %get-tuple-element.88.place, f32[16,2,8,256]{3,2,1,0:T(8,128)S(1)} %all_to_all.38.near, f32[16,2,8,256]{3,2,1,0:T(8,128)S(1)} %collective-permute-done.3.far, f32[256,256]{1,0:T(8,128)S(1)} %copy-done.11, ...), custom_call_target="tpu_custom_call" | custom-call | flops 600000000 | bytes 2000000 | tf_op jit(solution)/shard_map/cond/branch_1_fun/pallas_call | solution.py:282
  144.1 0.0 copy-start.14
  144.1 0.0 copy-start.15
  144.1 0.7 copy-done.14
  144.8 0.0 copy-done.15
  (3 shorter events, 0.0 us)
Async XLA Ops:
  5.9 57.4 %copy-start.5 = (f32[1536,256]{1,0:T(8,128)S(1)}, f32[1536,256]{1,0:T(8,128)}, u32[]{:S(2)}) copy-start(f32[1536,256]{1,0:T(8,128)} %get-tuple-element.91.panel_two) | copy-start | bytes 4718596 | tf_op jit(solution)/shard_map/cond
  8.5 54.8 %copy-start.3 = (f32[1536,256]{1,0:T(8,128)S(1)}, f32[1536,256]{1,0:T(8,128)}, u32[]{:S(2)}) copy-start(f32[1536,256]{1,0:T(8,128)} %get-tuple-element.90.panel_one) | copy-start | bytes 4718596 | tf_op jit(solution)/shard_map/cond
  8.5 54.8 %copy-start.7 = (f32[256,256]{1,0:T(8,128)S(1)}, f32[256,256]{1,0:T(8,128)}, u32[]{:S(2)}) copy-start(f32[256,256]{1,0:T(8,128)} %get-tuple-element.93.lower_one) | copy-start | bytes 786436 | tf_op jit(solution)/shard_map/cond
  8.5 54.8 %copy-start.8 = (f32[256,256]{1,0:T(8,128)S(1)}, f32[256,256]{1,0:T(8,128)}, u32[]{:S(2)}) copy-start(f32[256,256]{1,0:T(8,128)} %get-tuple-element.94.lower_two) | copy-start | bytes 786436 | tf_op jit(solution)/shard_map/cond
  8.5 54.8 %copy-start.9 = (f32[2,192,16]{2,1,0:T(8,128)S(1)}, f32[2,192,16]{2,1,0:T(8,128)}, u32[]{:S(2)}) copy-start(f32[2,192,16]{2,1,0:T(8,128)} %get-tuple-element.95.slots_t) | copy-start | bytes 73732 | tf_op jit(solution)/shard_map/cond
  8.5 7.1 %collective-permute-start = (f32[112,256]{1,0:T(8,128)S(1)}, f32[112,256]{1,0:T(8,128)S(1)}, u32[]{:S(2)}, u32[]{:S(2)}) collective-permute-start(f32[112,256]{1,0:T(8,128)S(1)} %branch_1_fun.5), channel_id=1, source_target_pairs={{0,0},{1,16},{2,32},{3,48},{4,64},{5,80},{6,96},{7,112},{8,128},{9... | collective-permute-start | bytes 344072 | tf_op jit(solution)/shard_map/cond/branch_1_fun/ppermute | solution.py:391
  61.0 4.3 %collective-permute-start.1 = (f32[8,112,256]{2,1,0:T(8,128)S(1)}, f32[8,112,256]{2,1,0:T(8,128)S(1)}, u32[]{:S(2)}, u32[]{:S(2)}) collective-permute-start(f32[8,112,256]{2,1,0:T(8,128)S(1)} %all_to_all.35.own), channel_id=1, source_target_pairs={{0,16},{16,0},{32,48},{48,32},{64,80},{80,64},{96,112},{112,96},{1... | collective-permute-start | bytes 2752520 | tf_op jit(solution)/shard_map/cond/branch_1_fun/ppermute | solution.py:394
  79.0 1.6 %collective-permute-start.2 = (f32[16,16,256]{2,1,0:T(8,128)S(1)}, f32[16,16,256]{2,1,0:T(8,128)S(1)}, u32[]{:S(2)}, u32[]{:S(2)}) collective-permute-start(f32[16,16,256]{2,1,0:T(8,128)S(1)} %get-tuple-element.99), channel_id=1, source_target_pairs={{0,16},{16,0},{32,48},{48,32},{64,80},{80,64},{96,112},{112,96},{1... | collective-permute-start | bytes 786440 | tf_op jit(solution)/shard_map/cond/branch_1_fun/ppermute | solution.py:396
  114.1 27.6 %copy-start.11 = (f32[256,256]{1,0:T(8,128)S(1)}, f32[256,256]{1,0:T(8,128)}, u32[]{:S(2)}) copy-start(f32[256,256]{1,0:T(8,128)} %get-tuple-element.102.pivot_one) | copy-start | bytes 786436 | tf_op jit(solution)/shard_map/cond
  114.1 27.6 %copy-start.13 = (f32[256,256]{1,0:T(8,128)S(1)}, f32[256,256]{1,0:T(8,128)}, u32[]{:S(2)}) copy-start(f32[256,256]{1,0:T(8,128)} %get-tuple-element.103.pivot_two) | copy-start | bytes 786436 | tf_op jit(solution)/shard_map/cond
  136.8 4.8 %collective-permute-start.3 = (f32[16,2,8,256]{3,2,1,0:T(8,128)S(1)}, f32[16,2,8,256]{3,2,1,0:T(8,128)S(1)}, u32[]{:S(2)}, u32[]{:S(2)}) collective-permute-start(f32[16,2,8,256]{3,2,1,0:T(8,128)S(1)} %all_to_all.38.near), channel_id=1, source_target_pairs={{0,16},{16,0},{32,48},{48,32},{64,80},{80,64},{96,112},{112,96},{1... | collective-permute-start | bytes 786440 | tf_op jit(solution)/shard_map/cond/branch_1_fun/ppermute | solution.py:387
  144.1 0.7 copy-start.14
  144.1 0.7 copy-start.15

commit v3 on v2

--- a/solution.py
+++ b/solution.py
@@ -16,6 +16,7 @@
 PIECE = 96
 SLOTS = 112
 PAIR = 2 * PIECE
+QUAD = 4 * PIECE
 WIDE = 256
 WINDOW = 16 * PIECE + 128
 
@@ -43,15 +44,28 @@
     return lax.dot_general(left, right, dims, preferred_element_type=F32)
 
 
-def tables_kernel(place, rows_one, rows_two, slots, slots_t, counts):
+def served(place):
+    return place[0] // 2 * 2 + place[1] % 2
+
+
+def tables_kernel(place, rows_one, rows_two, slots, slots_t, longest):
     row_at = lax.broadcasted_iota(jnp.int32, (PAIR, PAIR), 0)
     col_at = lax.broadcasted_iota(jnp.int32, (PAIR, PAIR), 1)
     near = (row_at >= PIECE) == (col_at >= PIECE)
     together = jnp.where(near, 1.0, 0.0).astype(BF16)
     earlier = jnp.where(near & (row_at < col_at), 1.0, 0.0).astype(BF16)
     same = jnp.where(row_at == col_at, 1.0, 0.0).astype(BF16)
-    before = jnp.where(lax.broadcasted_iota(jnp.int32, (16, PAIR), 1) >= PIECE, float(SLOTS), 0.0)
+    before = jnp.where(lax.broadcasted_iota(jnp.int32, (24, PAIR), 1) >= PIECE, float(SLOTS), 0.0)
+    ahead = jnp.where(row_at < col_at, 1.0, 0.0).astype(BF16)
+    pair_at = lax.broadcasted_iota(jnp.int32, (24, 24), 0)
+    other_at = lax.broadcasted_iota(jnp.int32, (24, 24), 1)
+    in_quad = pair_at // 2 == other_at // 2
+    earlier_pair = jnp.where(in_quad & (other_at < pair_at), 1.0, 0.0).astype(BF16)
+    quad = jnp.where(in_quad, 1.0, 0.0).astype(BF16)
+    quad_before = 0.0
+    own = lax.broadcasted_iota(jnp.int32, (24, PAIR), 0) < 8
     length = 0.0
+    blocks = [place[0], place[1], served(place)]
     slots[...] = jnp.full(slots.shape, -1.0, F32)
     for at, rows in enumerate((rows_one, rows_two)):
         index = rows[...]
@@ -60,20 +74,28 @@
             one_hot(lax.shift_right_logical(piece, 4), 16), one_hot(lax.bitwise_and(piece, 15), 16), NT
         )
         marks = []
-        for which in range(2):
-            first = jnp.sum(jnp.where(index < 16 * PIECE * place[which], 1.0, 0.0)).astype(jnp.int32)
+        for which in range(3):
+            first = jnp.sum(jnp.where(index < 16 * PIECE * blocks[which], 1.0, 0.0)).astype(jnp.int32)
             first = jnp.minimum(first // 128 * 128, index.shape[1] - WINDOW)
             some = rows[:, pl.ds(pl.multiple_of(first, 128), WINDOW)]
             pair = lax.shift_right_logical(piece_of(some), 1)
-            inner = jnp.where(lax.shift_right_logical(pair, 3) == place[which], lax.bitwise_and(pair, 7), -1)
+            inner = jnp.where(lax.shift_right_logical(pair, 3) == blocks[which], lax.bitwise_and(pair, 7), -1)
             marks.append(one_dot(one_hot(inner, 16), one_hot(some - PAIR * pair, PAIR), NT)[:8])
         marks = jnp.concatenate(marks, axis=0)
         marks_low = marks.astype(BF16)
-        slot = jnp.where(marks > 0.5, one_dot(marks_low, earlier) + before, -1.0)
+        total = lambda x: jnp.sum(x, axis=1, keepdims=True)
+        in_piece = one_dot(marks_low, earlier) + before
+        in_list = one_dot(marks_low, ahead) + (total(one_dot(earlier_pair, marks_low)) + quad_before)
         before = before + one_dot(marks_low, together)
+        quad_before = quad_before + total(one_dot(quad, marks_low))
+        slot = jnp.where(marks > 0.5, jnp.where(own, in_piece, in_list), -1.0)
         slots[:, WIDE * at:WIDE * at + PAIR] = slot
-        slots_t[at] = one_dot(same, slot.astype(BF16), NT)
-    counts[...] = length
+        high, low = split(slot)
+        slots_t[at] = one_dot(same, high, NT) + one_dot(same, low, NT)
+    gather = lax.broadcasted_iota(jnp.int32, (16, 16), 0) // 4 == lax.broadcasted_iota(jnp.int32, (16, 16), 1)
+    lists = one_dot(length.astype(BF16), jnp.where(gather, 1.0, 0.0).astype(BF16))
+    over = jnp.maximum(jnp.max(length) - SLOTS, jnp.max(lists) - QUAD)
+    longest[0] = over.astype(jnp.int32)
 
 
 def piece_of(index):
@@ -85,12 +107,12 @@
     return pl.pallas_call(
         tables_kernel,
         out_shape=[
-            jax.ShapeDtypeStruct((16, 2 * WIDE), F32),
-            jax.ShapeDtypeStruct((2, PAIR, 16), F32),
-            jax.ShapeDtypeStruct((16, 16), F32),
+            jax.ShapeDtypeStruct((24, 2 * WIDE), F32),
+            jax.ShapeDtypeStruct((2, PAIR, 24), F32),
+            jax.ShapeDtypeStruct((1,), jnp.int32),
         ],
         in_specs=[pl.BlockSpec(memory_space=pltpu.SMEM)] + [vmem] * 2,
-        out_specs=[vmem] * 3,
+        out_specs=[vmem] * 2 + [pl.BlockSpec(memory_space=pltpu.SMEM)],
         compiler_params=pltpu.CompilerParams(vmem_limit_bytes=24 << 20),
         cost_estimate=pl.CostEstimate(flops=200_000_000, bytes_accessed=300_000, transcendentals=0),
     )(place, rows_one[None, :], rows_two[None, :])
@@ -133,25 +155,78 @@
     return one_dot(chosen, hi) + one_dot(chosen, lo)
 
 
-def piece_kernel(place, panel_one, panel_two, slots, lower_one, lower_two, out):
-    at = place[1] % 2 * 8 + place[1] // 2
-    rows = pl.ds(pl.multiple_of(at * PIECE, PIECE), PIECE)
-    one = dot3(split(panel_one[rows, :]), split(lower_one[...]))
-    two = dot3(split(panel_two[rows, :]), split(lower_two[...]))
-    chosen = chosen_rows(slots[pl.ds(at // 2, 1), :], at % 2 * SLOTS, SLOTS)
-    out[...] = pack(chosen, jnp.concatenate([one, one], axis=0), jnp.concatenate([two, two], axis=0))
-
-
-def packed_piece(place, panel_one, panel_two, slots, lower_one, lower_two):
+def quad_copies(panels, at, into, arrived):
+    first = pl.multiple_of(at // 4 * QUAD, QUAD)
+    return [
+        pltpu.make_async_copy(panel.at[pl.ds(first, QUAD), :], to, arrived.at[i])
+        for i, (panel, to) in enumerate(zip(panels, into))
+    ]
+
+
+def quad_kernel(place, panel_one, panel_two, out_one, out_two, arrived):
+    at = (1 - place[0] % 2) * 8 + place[1] // 2
+    copies = quad_copies((panel_one, panel_two), at, (out_one, out_two), arrived)
+    for copy in copies:
+        copy.start()
+    for copy in copies:
+        copy.wait()
+
+
+def quads(place, panel_one, panel_two):
+    vmem = pl.BlockSpec(memory_space=pltpu.VMEM)
+    return pl.pallas_call(
+        quad_kernel,
+        out_shape=[jax.ShapeDtypeStruct((QUAD, panel_one.shape[1]), F32)] * 2,
+        in_specs=[pl.BlockSpec(memory_space=pltpu.SMEM)] + [pl.BlockSpec(memory_space=pl.ANY)] * 2,
+        out_specs=[vmem] * 2,
+        scratch_shapes=[pltpu.SemaphoreType.DMA((2,))],
+        compiler_params=pltpu.CompilerParams(vmem_limit_bytes=8 << 20),
+        cost_estimate=pl.CostEstimate(flops=0, bytes_accessed=1_600_000, transcendentals=0),
+    )(place, panel_one, panel_two)
+
+
+def piece_kernel(
+    place, panel_one, panel_two, given_one, given_two, slots, lower_one, lower_two, out, raw_one, raw_two, arrived
+):
+    at = place[0] % 2 * 8 + place[1] // 2
+    mine = place[0] % 2 == place[1] % 2
+
+    @pl.when(mine)
+    def _():
+        copies = quad_copies((panel_one, panel_two), at, (raw_one, raw_two), arrived)
+        for copy in copies:
+            copy.start()
+        for copy in copies:
+            copy.wait()
+
+    @pl.when(jnp.logical_not(mine))
+    def _():
+        raw_one[...] = given_one[...]
+        raw_two[...] = given_two[...]
+
+    one = dot3(split(raw_one[...]), split(lower_one[...]))
+    two = dot3(split(raw_two[...]), split(lower_two[...]))
+    packed = 0.0
+    for pair in range(2):
+        rows = slice(PAIR * pair, PAIR * pair + PAIR)
+        chosen = chosen_rows(slots[pl.ds(16 + at // 4 * 2 + pair, 1), :], at % 4 * PIECE, PIECE)
+        packed = packed + pack(chosen, one[rows], two[rows])
+    for copy in range(out.shape[0]):
+        out[copy] = packed
+
+
+def packed_piece(place, panel_one, panel_two, given, slots, lower_one, lower_two, copies):
+    sn = lower_one.shape[0]
     vmem = pl.BlockSpec(memory_space=pltpu.VMEM)
     return pl.pallas_call(
         piece_kernel,
-        out_shape=jax.ShapeDtypeStruct((SLOTS, lower_one.shape[0]), F32),
-        in_specs=[pl.BlockSpec(memory_space=pltpu.SMEM)] + [vmem] * 5,
+        out_shape=jax.ShapeDtypeStruct((copies, PIECE, sn), F32),
+        in_specs=[pl.BlockSpec(memory_space=pltpu.SMEM)] + [pl.BlockSpec(memory_space=pl.ANY)] * 2 + [vmem] * 5,
         out_specs=vmem,
+        scratch_shapes=[pltpu.VMEM((QUAD, sn), F32)] * 2 + [pltpu.SemaphoreType.DMA((2,))],
         compiler_params=pltpu.CompilerParams(vmem_limit_bytes=16 << 20),
-        cost_estimate=pl.CostEstimate(flops=200_000_000, bytes_accessed=2_000_000, transcendentals=0),
-    )(place, panel_one, panel_two, slots, lower_one, lower_two)
+        cost_estimate=pl.CostEstimate(flops=500_000_000, bytes_accessed=2_000_000, transcendentals=0),
+    )(place, panel_one, panel_two, *given, slots, lower_one, lower_two)
 
 
 def packed_front_kernel(
@@ -172,14 +247,14 @@
     for at, ref in enumerate((own, other)):
         whose = core if at == 0 else 1 - core
         slot = [jnp.where(whose == 0, slots_t[which, :, 8:12], slots_t[which, :, 12:16]) for which in range(2)]
-        for q in range(4):
-            spot = [place_rows(slot[which][:, q:q + 1], 2 * SLOTS) for which in range(2)]
-            parts = jnp.concatenate(split(ref[2 * q:2 * q + 2].reshape(2 * SLOTS, sn)), axis=1)
+        for q in range(2):
+            spot = [place_rows(slot[which][:, 2 * q + e:2 * q + e + 1], QUAD) for which in range(2) for e in range(2)]
+            parts = jnp.concatenate(split(ref[4 * q:4 * q + 4].reshape(QUAD, sn)), axis=1)
             rows = one_dot(jnp.concatenate(spot, axis=0), parts).astype(BF16)
-            into = pl.ds(pl.multiple_of(whose * half + PAIR * q, PAIR), PAIR)
+            into = pl.ds(pl.multiple_of(whose * half + QUAD * q, QUAD), QUAD)
             for which in range(2):
-                s_hi[into, sn * which:sn * which + sn] = rows[PAIR * which:PAIR * which + PAIR, :sn]
-                s_lo[into, sn * which:sn * which + sn] = rows[PAIR * which:PAIR * which + PAIR, sn:]
+                s_hi[into, sn * which:sn * which + sn] = rows[QUAD * which:QUAD * which + QUAD, :sn]
+                s_lo[into, sn * which:sn * which + sn] = rows[QUAD * which:QUAD * which + QUAD, sn:]
     diag[...] = jnp.zeros_like(diag)
 
     for step in range(STEPS):
@@ -272,8 +347,9 @@
                 sums[at, pl.ds(pl.multiple_of((2 * d + whose) * share, share), share), :] = ref[d, at]
     first = pivot_one[...] + sums[0]
     inverse_one[...] = first
-    panel_two[...] = -matmul(product_two[...], first)
-    inverse_two[...] = pivot_two[...] + matmul(first.T, matmul(sums[1], first))
+    parts = split(first)
+    panel_two[...] = -dot3(split(product_two[...]), parts)
+    inverse_two[...] = pivot_two[...] + dot3(split(first.T), split(dot3(split(sums[1]), parts)))
 
 
 def finish(place, near, far, pivot_one, pivot_two, product_two):
@@ -377,20 +453,21 @@
     def spread(x, axis, copies, groups=None):
         return exchange(jnp.broadcast_to(x, (copies,) + x.shape), axis, groups)
 
-    turn = [(r * n + c, c * n + r) for r in range(n) for c in range(n)]
     place = jnp.stack([row, col])
-    slots, slots_t, counts = list_tables(place, rows_one, rows_two)
+    at = core * half + col // 2
+
+    given = [lax.ppermute(q, "row", swap) for q in quads(place, panel_one, panel_two)]
+    slots, slots_t, longest = list_tables(place, rows_one, rows_two)
 
     def complete(keep, product_two):
         keep = jnp.sum(spread(keep, "row", half, parities), axis=0)
         near = spread(keep, "col", n)
         return finish(place, near, lax.ppermute(near, "row", swap), pivot_one, pivot_two, product_two)
 
-    def packed(place, front, slots, slots_t):
-        mine = packed_piece(place, panel_one, panel_two, slots, lower_one, lower_two)
-        mine = lax.ppermute(mine, ("row", "col"), turn)
+    def packed(place, given, front, slots, slots_t):
+        mine = packed_piece(place, panel_one, panel_two, given, slots, lower_one, lower_two, half)
+        own = exchange(exchange(mine, "row", parities), "col", parities)
         st_hi, st_lo = local_solved(slots_t, panel_one, panel_two, lower_one, lower_two)
-        own = spread(mine, "row", half, parities)
         other = lax.ppermute(own, "row", swap)
         parts, give = packed_front_product(place, front, own, other, slots_t, slots, st_hi, st_lo, n)
         shares = parts[:, SLOTS:] + lax.ppermute(give, "row", swap)
@@ -398,18 +475,21 @@
         inverse_one, product_two, keep = summed_piece(place, parts, slots_t)
         return inverse_one, *complete(keep.reshape(2, sn // n // 2, sn), product_two)
 
-    def dense(place, front, slots, slots_t):
-        at = (col % 2 * half + col // 2) * piece
+    def dense(place, given, front, slots, slots_t):
+        first = served(place) * block + at * piece
+        got = [
+            jnp.where(core == col % 2, lax.dynamic_slice_in_dim(p, at // 4 * 4 * piece, 4 * piece, 0), g)
+            for p, g in zip((panel_one, panel_two), given)
+        ]
         solved = jnp.concatenate(
             [
-                matmul(marked(rows, row * block + at, piece) * lax.dynamic_slice_in_dim(panel, at, piece, 0), lower)
-                for rows, panel, lower in ((rows_one, panel_one, lower_one), (rows_two, panel_two, lower_two))
+                matmul(marked(rows, first, piece) * lax.dynamic_slice_in_dim(r, at % 4 * piece, piece, 0), lower)
+                for rows, r, lower in ((rows_one, got[0], lower_one), (rows_two, got[1], lower_two))
             ],
             axis=1,
         )
-        solved = lax.ppermute(solved, ("row", "col"), turn)
         st_hi, st_lo = local_solved(slots_t, panel_one, panel_two, lower_one, lower_two)
-        own = spread(solved, "row", half, parities).reshape(block // 2, 2 * sn)
+        own = exchange(spread(solved, "row", half, parities), "col", parities).reshape(block // 2, 2 * sn)
         other = lax.ppermute(own, "row", swap)
         parts = front_product(core[None], front, own, other, st_hi, st_lo, n)
         summed = jnp.sum(exchange(parts, "col"), axis=0)
@@ -420,7 +500,13 @@
         inverse_one = -(marked(rows_one, mine, piece) * summed[:piece, :sn])
         return inverse_one, *complete(keep, marked(rows_two, mine, piece) * summed[:piece, sn:])
 
-    return lax.cond(jnp.max(counts) <= SLOTS, packed, dense, place, front, slots, slots_t)
+    results = packed(place, given, front, slots, slots_t)
+    return lax.cond(
+        longest[0] <= 0,
+        lambda results, *_: results,
+        lambda results, *rest: dense(*rest),
+        results, place, given, front, slots, slots_t,
+    )
 
 
 def solution(mesh):

time: 145 us -> 143 us (0.986)
  waiting for transfers between devices: 5.09 us -> 1.87 us
    ppermute x1 -> x2, waiting for transfers between devices: 2.46 us -> 0.01 us  [per_device(): lax.ppermute(q, 'row', swap)]
    ppermute x1, starting transfers between devices: 2.22 us -> 3.83 us  [packed(): other = lax.ppermute(own, 'row', swap)]
    pallas_call x2 -> x3, Pallas kernels: 6.29 us -> 7.79 us  [the longest x1 4.33 us: list_tables(): pl.pallas_call(tables_kernel, out_shape=[jax.ShapeDtypeStruct((24, 2 * WI...]
    ppermute x1 -> x2, starting transfers between devices: 4.64 us -> 3.43 us  [per_device(): lax.ppermute(q, 'row', swap)]
    all_to_all x4 -> x5, blocking collectives: 99.9 us -> 100 us  [exchange(): return lax.all_to_all(x, axis, 0, 0, axis_index_groups=groups)]
  transfers between devices with their start and end apart: 4 -> 5, of which waited for: 4 -> 3; matrix products, arithmetic and copies ran while one was open for 0% -> 0% of each run, Pallas kernels for 1% -> 4%
where the time goes in v3:
time: 143 us
  blocking collectives  100 us (70%)
  Pallas kernels  26.6 us (19%)
  starting transfers between devices  11.4 us (8%)
  waiting for transfers between devices  1.87 us (1%)
  between operations  1.47 us (1%)
    all_to_all x5, blocking collectives, exchange(): return lax.all_to_all(x, axis, 0, 0, axis_index_groups=groups)  100 us
    pallas_call x1, Pallas kernels, packed_front_product(): pl.pallas_call(packed_front_kernel, out_shape=[jax.ShapeDtypeStruct((col_...  13.1 us
    pallas_call x1, Pallas kernels, list_tables(): pl.pallas_call(tables_kernel, out_shape=[jax.ShapeDtypeStruct((24, 2 * WI...  4.33 us
    ppermute x1, starting transfers between devices, packed(): other = lax.ppermute(own, 'row', swap)  3.83 us
    ppermute x1, starting transfers between devices, complete(): lax.ppermute(near, 'row', swap)  3.68 us
    ppermute x2, starting transfers between devices, per_device(): lax.ppermute(q, 'row', swap)  3.43 us
  transfers between devices with their start and end apart: 5, of which 3 were waited for; matrix products, arithmetic and copies ran while one was open for 0% of the time, Pallas kernels for 4%

profile of v3, /device:TPU:1, one launch (start us, length us, event | category | flops | bytes accessed | tf_op | source)
XLA Modules:
  0.0 142.5 jit_solution(4800689579111450007)
XLA Ops:
  0.6 0.1 pad_add_fusion.place
  0.7 0.0 copy-start.13
  0.7 0.0 copy-start.2
  0.7 0.0 copy-start.3
  0.7 0.0 copy-start.5
  0.7 0.0 copy-start.6
  0.7 2.0 %shard_map.123 = (f32[384,256]{1,0:T(8,128)S(1)}, f32[384,256]{1,0:T(8,128)S(1)}) custom-call(s32[2]{0:T(128)S(1)} %pad_add_fusion.place, f32[1536,256]{1,0:T(8,128)} %panel_one.5, f32[1536,256]{1,0:T(8,128)} %panel_two.5), custom_call_target="tpu_custom_call" | custom-call | bytes 1600000 | tf_op jit(solution)/shard_map/pallas_call | solution.py:177
  2.7 3.3 %collective-permute-start.3 = (f32[384,256]{1,0:T(8,128)S(1)}, f32[384,256]{1,0:T(8,128)S(1)}, u32[]{:S(2)}, u32[]{:S(2)}) collective-permute-start(f32[384,256]{1,0:T(8,128)S(1)} %get-tuple-element.137), channel_id=1, source_target_pairs={{0,16},{16,0},{32,48},{48,32},{64,80},{80,64},{96,112},{112,96},{1... | collective-permute-start | bytes 1179656 | tf_op jit(solution)/shard_map/ppermute | solution.py:459
  6.0 0.1 collective-permute-start.4
  6.1 4.3 %shard_map.122 = (f32[24,512]{1,0:T(8,128)S(1)}, f32[2,192,24]{2,1,0:T(8,128)S(1)}, s32[1]{0:T(128)}) custom-call(s32[2]{0:T(128)S(1)} %pad_add_fusion.place, s32[1,12288]{1,0:T(1,128)} %bitcast.24, s32[1,8192]{1,0:T(1,128)} %bitcast.25), custom_call_target="tpu_custom_call" | custom-call | flops 200000000 | bytes 300000 | tf_op jit(solution)/shard_map/pallas_call | solution.py:107
  10.5 0.0 copy-start.10
  10.5 0.0 collective-permute-done.3.given_one
  10.5 0.0 copy-start.8
  10.5 0.0 collective-permute-done.4.given_two
  10.5 0.0 copy-start.9
  10.5 0.0 copy-done.2
  10.5 0.0 copy-done.3
  10.6 0.0 copy-done.5
  10.6 0.0 copy-done.6
  10.6 1.5 %shard_map.124 = f32[8,96,256]{2,1,0:T(8,128)S(1)} custom-call(s32[2]{0:T(128)S(1)} %pad_add_fusion.place, f32[1536,256]{1,0:T(8,128)S(1)} %copy-done.2, f32[1536,256]{1,0:T(8,128)S(1)} %copy-done.3, f32[384,256]{1,0:T(8,128)S(1)} %collective-permute-done.3.given_one, f32[384,256]{1,0:T(8,128)S(1)} %collective-permute-done.4.given_two, ...), custom_call_target="tpu_custom_call" | custom-call | flops 500000000 | bytes 2000000 | tf_op jit(solution)/shard_map/pallas_call | solution.py:221
  12.1 0.0 copy-done.8
  12.1 0.0 copy-done.9
  12.1 0.0 copy-start.15
  12.1 27.9 %all_to_all.49 = f32[8,96,256]{2,1,0:T(8,128)S(1)} all-to-all(f32[8,96,256]{2,1,0:T(8,128)S(1)} %shard_map.124), channel_id=1, replica_groups={{0,32,64,96,128,160,192,224},{16,48,80,112,144,176,208,240},{1,33,65,97..., dimensions={0} | all-to-all | bytes 1572864 | tf_op jit(solution)/shard_map/all_to_all | solution.py:451
  40.0 18.0 %all_to_all.50.own = f32[8,96,256]{2,1,0:T(8,128)S(1)} all-to-all(f32[8,96,256]{2,1,0:T(8,128)S(1)} %all_to_all.49), channel_id=1, replica_groups={{0,2,4,6,8,10,12,14},{1,3,5,7,9,11,13,15},{16,18,20,22,24,26,28,30},{17..., dimensions={0} | all-to-all | bytes 1572864 | tf_op jit(solution)/shard_map/all_to_all | solution.py:451
  58.0 3.8 %collective-permute-start.5 = (f32[8,96,256]{2,1,0:T(8,128)S(1)}, f32[8,96,256]{2,1,0:T(8,128)S(1)}, u32[]{:S(2)}, u32[]{:S(2)}) collective-permute-start(f32[8,96,256]{2,1,0:T(8,128)S(1)} %all_to_all.50.own), channel_id=1, source_target_pairs={{0,16},{16,0},{32,48},{48,32},{64,80},{80,64},{96,112},{112,96},{1... | collective-permute-start | bytes 2359304 | tf_op jit(solution)/shard_map/ppermute | solution.py:471
  61.8 1.7 %shard_map.125 = (bf16[2,256,1536]{2,1,0:T(8,128)(2,1)S(1)}, bf16[2,256,1536]{2,1,0:T(8,128)(2,1)S(1)}) custom-call(f32[2,192,24]{2,1,0:T(8,128)S(1)} %get-tuple-element.139.slots_t, f32[1536,256]{1,0:T(8,128)S(1)} %copy-done.2, f32[1536,256]{1,0:T(8,128)S(1)} %copy-done.3, f32[256,256]{1,0:T(8,128)S(1)} %copy-done.5, f32[256,256]{1,0:T(8,128)S(1)} %copy-done.6), custom_call_target="tpu_custom_call" | custom-call | flops 2000000000 | bytes 6000000 | tf_op jit(solution)/shard_map/pallas_call | solution.py:131
  63.6 0.2 collective-permute-done.5.other
  63.7 0.0 copy-done.15
  63.7 13.1 %shard_map.126 = (f32[16,128,256]{2,1,0:T(8,128)S(1)}, f32[16,16,256]{2,1,0:T(8,128)S(1)}) custom-call(s32[2]{0:T(128)S(1)} %pad_add_fusion.place, f32[1536,1536]{1,0:T(8,128)S(1)} %copy-done.15, f32[8,96,256]{2,1,0:T(8,128)S(1)} %all_to_all.50.own, f32[8,96,256]{2,1,0:T(8,128)S(1)} %collective-permute-done.5.other, ...), custom_call_target="tpu_custom_call" | custom-call | flops 7247757312 | bytes 20000000 | tf_op jit(solution)/shard_map/pallas_call | solution.py:287
  76.8 0.5 collective-permute-start.6
  77.3 1.2 collective-permute-done.6
  78.5 0.1 add_dynamic-update-slice_fusion
  78.5 32.2 %all_to_all.51.parts = f32[16,128,256]{2,1,0:T(8,128)S(1)} all-to-all(f32[16,128,256]{2,1,0:T(8,128)S(1)} %add_dynamic-update-slice_fusion), channel_id=1, replica_groups=mesh['row'=16,'col'=16] {'col'}, dimensions={0} | all-to-all | bytes 4194304 | tf_op jit(solution)/shard_map/all_to_all | solution.py:451
  110.7 0.0 copy-done.13
  110.7 0.0 copy-done.10
  110.7 1.5 %shard_map.127 = (f32[96,256]{1,0:T(8,128)}, f32[96,256]{1,0:T(8,128)S(1)}, f32[16,256]{1,0:T(8,128)S(1)}) custom-call(s32[2]{0:T(128)S(1)} %pad_add_fusion.place, f32[16,128,256]{2,1,0:T(8,128)S(1)} %all_to_all.51.parts, f32[2,192,24]{2,1,0:T(8,128)S(1)} %get-tuple-element.139.slots_t), custom_call_target="tpu_custom_call" | custom-call | flops 100000000 | bytes 3000000 | tf_op jit(solution)/shard_map/pallas_call | solution.py:331
  112.3 11.0 %all_to_all.52 = f32[8,2,8,256]{3,2,1,0:T(8,128)} all-to-all(f32[8,2,8,256]{3,2,1,0:T(8,128)S(1)} %broadcast_in_dim.34), channel_id=1, replica_groups={{0,32,64,96,128,160,192,224},{16,48,80,112,144,176,208,240},{1,33,65,97..., dimensions={0} | all-to-all | bytes 262144 | tf_op jit(solution)/shard_map/all_to_all | solution.py:451
  123.3 0.9 reduce_sum.27
  124.2 0.0 copy-start.12
  124.2 11.0 %all_to_all.53.near = f32[16,2,8,256]{3,2,1,0:T(8,128)S(1)} all-to-all(f32[16,2,8,256]{3,2,1,0:T(8,128)S(1)} %broadcast_in_dim.35), channel_id=1, replica_groups=mesh['row'=16,'col'=16] {'col'}, dimensions={0} | all-to-all | bytes 524288 | tf_op jit(solution)/shard_map/all_to_all | solution.py:451
  135.2 3.7 %collective-permute-start.7 = (f32[16,2,8,256]{3,2,1,0:T(8,128)S(1)}, f32[16,2,8,256]{3,2,1,0:T(8,128)S(1)}, u32[]{:S(2)}, u32[]{:S(2)}) collective-permute-start(f32[16,2,8,256]{3,2,1,0:T(8,128)S(1)} %all_to_all.53.near), channel_id=1, source_target_pairs={{0,16},{16,0},{32,48},{48,32},{64,80},{80,64},{96,112},{112,96},{1... | collective-permute-start | bytes 786440 | tf_op jit(solution)/shard_map/ppermute | solution.py:465
  139.6 0.5 collective-permute-done.7.far
  140.1 2.5 %shard_map.128 = (f32[256,256]{1,0:T(8,128)}, f32[96,256]{1,0:T(8,128)}, f32[256,256]{1,0:T(8,128)}) custom-call(s32[2]{0:T(128)} %copy-done.13, f32[16,2,8,256]{3,2,1,0:T(8,128)S(1)} %all_to_all.53.near, f32[16,2,8,256]{3,2,1,0:T(8,128)S(1)} %collective-permute-done.7.far, f32[256,256]{1,0:T(8,128)} %pivot_one.1, f32[256,256]{1,0:T(8,128)} %pivot_two.1, ...), custom_call_target="tpu_custom_call" | custom-call | flops 600000000 | bytes 2000000 | tf_op jit(solution)/shard_map/pallas_call | solution.py:358
  142.5 0.0 copy-done.12
  (3 shorter events, 0.0 us)
Async XLA Ops:
  0.7 110.0 %copy-start.13 = (s32[2]{0:T(128)}, s32[2]{0:T(128)S(1)}, u32[]{:S(2)}) copy-start(s32[2]{0:T(128)S(1)} %pad_add_fusion.place) | copy-start | bytes 28
  0.7 9.8 %copy-start.2 = (f32[1536,256]{1,0:T(8,128)S(1)}, f32[1536,256]{1,0:T(8,128)}, u32[]{:S(2)}) copy-start(f32[1536,256]{1,0:T(8,128)} %panel_one.5) | copy-start | bytes 4718596
  0.7 9.8 %copy-start.3 = (f32[1536,256]{1,0:T(8,128)S(1)}, f32[1536,256]{1,0:T(8,128)}, u32[]{:S(2)}) copy-start(f32[1536,256]{1,0:T(8,128)} %panel_two.5) | copy-start | bytes 4718596
  0.7 9.8 %copy-start.5 = (f32[256,256]{1,0:T(8,128)S(1)}, f32[256,256]{1,0:T(8,128)}, u32[]{:S(2)}) copy-start(f32[256,256]{1,0:T(8,128)} %lower_one.3) | copy-start | bytes 786436
  0.7 9.8 %copy-start.6 = (f32[256,256]{1,0:T(8,128)S(1)}, f32[256,256]{1,0:T(8,128)}, u32[]{:S(2)}) copy-start(f32[256,256]{1,0:T(8,128)} %lower_two.3) | copy-start | bytes 786436
  2.7 7.8 %collective-permute-start.3 = (f32[384,256]{1,0:T(8,128)S(1)}, f32[384,256]{1,0:T(8,128)S(1)}, u32[]{:S(2)}, u32[]{:S(2)}) collective-permute-start(f32[384,256]{1,0:T(8,128)S(1)} %get-tuple-element.137), channel_id=1, source_target_pairs={{0,16},{16,0},{32,48},{48,32},{64,80},{80,64},{96,112},{112,96},{1... | collective-permute-start | bytes 1179656 | tf_op jit(solution)/shard_map/ppermute | solution.py:459
  6.0 4.5 %collective-permute-start.4 = (f32[384,256]{1,0:T(8,128)S(1)}, f32[384,256]{1,0:T(8,128)S(1)}, u32[]{:S(2)}, u32[]{:S(2)}) collective-permute-start(f32[384,256]{1,0:T(8,128)S(1)} %get-tuple-element.138), channel_id=1, source_target_pairs={{0,16},{16,0},{32,48},{48,32},{64,80},{80,64},{96,112},{112,96},{1... | collective-permute-start | bytes 1179656 | tf_op jit(solution)/shard_map/ppermute | solution.py:459
  10.5 100.3 %copy-start.10 = (f32[2,192,24]{2,1,0:T(8,128)}, f32[2,192,24]{2,1,0:T(8,128)S(1)}, u32[]{:S(2)}) copy-start(f32[2,192,24]{2,1,0:T(8,128)S(1)} %get-tuple-element.139.slots_t) | copy-start | bytes 110596
  10.5 1.6 %copy-start.8 = (f32[384,256]{1,0:T(8,128)}, f32[384,256]{1,0:T(8,128)S(1)}, u32[]{:S(2)}) copy-start(f32[384,256]{1,0:T(8,128)S(1)} %collective-permute-done.3.given_one) | copy-start | bytes 1179652
  10.5 1.6 %copy-start.9 = (f32[384,256]{1,0:T(8,128)}, f32[384,256]{1,0:T(8,128)S(1)}, u32[]{:S(2)}) copy-start(f32[384,256]{1,0:T(8,128)S(1)} %collective-permute-done.4.given_two) | copy-start | bytes 1179652
  12.1 51.7 %copy-start.15 = (f32[1536,1536]{1,0:T(8,128)S(1)}, f32[1536,1536]{1,0:T(8,128)}, u32[]{:S(2)}) copy-start(f32[1536,1536]{1,0:T(8,128)} %front.1) | copy-start | bytes 28311556
  58.0 5.7 %collective-permute-start.5 = (f32[8,96,256]{2,1,0:T(8,128)S(1)}, f32[8,96,256]{2,1,0:T(8,128)S(1)}, u32[]{:S(2)}, u32[]{:S(2)}) collective-permute-start(f32[8,96,256]{2,1,0:T(8,128)S(1)} %all_to_all.50.own), channel_id=1, source_target_pairs={{0,16},{16,0},{32,48},{48,32},{64,80},{80,64},{96,112},{112,96},{1... | collective-permute-start | bytes 2359304 | tf_op jit(solution)/shard_map/ppermute | solution.py:471
  76.8 1.6 %collective-permute-start.6 = (f32[16,16,256]{2,1,0:T(8,128)S(1)}, f32[16,16,256]{2,1,0:T(8,128)S(1)}, u32[]{:S(2)}, u32[]{:S(2)}) collective-permute-start(f32[16,16,256]{2,1,0:T(8,128)S(1)} %get-tuple-element.144), channel_id=1, source_target_pairs={{0,16},{16,0},{32,48},{48,32},{64,80},{80,64},{96,112},{112,96},{1... | collective-permute-start | bytes 786440 | tf_op jit(solution)/shard_map/ppermute | solution.py:473
  124.2 18.3 %copy-start.12 = (s32[12288]{0:T(1024)S(1)}, s32[12288]{0:T(1024)}, u32[]{:S(2)}) copy-start(s32[12288]{0:T(1024)} %param.18) | copy-start | bytes 147460
  135.2 4.8 %collective-permute-start.7 = (f32[16,2,8,256]{3,2,1,0:T(8,128)S(1)}, f32[16,2,8,256]{3,2,1,0:T(8,128)S(1)}, u32[]{:S(2)}, u32[]{:S(2)}) collective-permute-start(f32[16,2,8,256]{3,2,1,0:T(8,128)S(1)} %all_to_all.53.near), channel_id=1, source_target_pairs={{0,16},{16,0},{32,48},{48,32},{64,80},{80,64},{96,112},{112,96},{1... | collective-permute-start | bytes 786440 | tf_op jit(solution)/shard_map/ppermute | solution.py:465
